TPU v7x, 128 devices: a whole 4x4x4 slice. The times are simulated.
128 devices in a mesh: tm: 32 (over x, z, y_lo), mode: 4 (over y_hi, core).
Axes of the slice: x: 4, y: 4 (y_hi: 2, y_lo: 2; y = y_hi * 2 + y_lo), z: 4, core: 2. Of those that a mesh axis runs over, the one named last changes fastest.
Arguments:
- field_codes: bfloat16 [2, 64, 2, 1024, 1024], P(None, 'tm', None, 'mode'), may hold values from -6 to 6
- scales: float32 [2, 64, 1024], P(None, 'tm', 'mode'), may hold values from 0.01 to 0.1
- mom_index: int32 [4], replicated, may hold values from 0 to 1
- separations: int32 [3], replicated, may hold values from 1 to 6, as said below
- source_slice: int32 [2048], P('tm'), may hold values from 0 to 63
- noise_left: bfloat16 [2048, 2, 1024], P('tm'), may hold values from -0.1875 to 0.1875
- noise_right: bfloat16 [2048, 2, 1024], P('tm', None, 'mode'), may hold values from -6 to 6
Outputs:
- box_trace: float32 [64, 3, 2], P('tm')
- cross_trace: float32 [64, 3, 2], P('tm')
- noise_trace: float32 [64, 3, 2], P('tm')
Inputs may be any that keep to these rules, and one draw needn't show every extreme that they name: The three separations lie one in 1 to 2, one in 3 to 4, and one equals 6, in an order drawn from the seed.
All inputs are finite; a program needn't handle non-finite values.
Results may differ from a plain program's by a relative error of at most 0.0072.
Values may be sent and summed in bfloat16 or wider, within the bound.
A program may use at most 256 MiB of HBM per device.

v0:
```python
import jax
import jax.numpy as jnp
from jax import lax
from jax.sharding import PartitionSpec as P


def shifted(x, axis, by):
    devices = lax.axis_size(axis)
    return lax.ppermute(x, axis, [(i, (i + by) % devices) for i in range(devices)])


def complex_product(left, right):
    pieces = jnp.einsum("tcak,tdkb->tcdab", left, right, preferred_element_type=jnp.float32)
    return jnp.stack([pieces[:, 0, 0] - pieces[:, 1, 1], pieces[:, 0, 1] + pieces[:, 1, 0]], axis=1)


def pair_table(rows_part, cols_part):
    pieces = jnp.einsum("tcij,sdji->tscd", rows_part, cols_part, preferred_element_type=jnp.float32)
    return jnp.stack(
        [pieces[..., 0, 0] - pieces[..., 1, 1], pieces[..., 0, 1] + pieces[..., 1, 0]], axis=-1
    )


def noise_table(weights, cols_part):
    pieces = jnp.einsum("tcik,sdik->tscd", weights, cols_part, preferred_element_type=jnp.float32)
    return jnp.stack(
        [pieces[..., 0, 0] - pieces[..., 1, 1], pieces[..., 0, 1] + pieces[..., 1, 0]], axis=-1
    )


def to_columns(rows_stack):
    return lax.all_to_all(rows_stack, "mode", split_axis=4, concat_axis=3, tiled=True)


def on_device(field_codes, scales, mom_index, separations, source_slice, noise_left, noise_right):
    moment_count = field_codes.shape[0]
    slices = field_codes.shape[1]
    fields = (field_codes.astype(jnp.float32) * scales[:, :, None, :, None]).astype(jnp.bfloat16)
    picked = []
    for insertion in range(4):
        running = jnp.zeros_like(fields[0])
        for moment in range(moment_count):
            running = running + jnp.where(
                mom_index[insertion] == moment, fields[moment], jnp.zeros_like(fields[0])
            )
        picked.append(running)
    first_field, second_field, third_field, fourth_field = picked
    pieces = (
        lax.all_gather(first_field, "mode", axis=2, tiled=True),
        lax.all_gather(third_field, "mode", axis=2, tiled=True),
    )
    left_product = complex_product(fourth_field, pieces[0])
    right_product = complex_product(second_field, pieces[1])
    left_product = left_product.astype(jnp.bfloat16)
    right_product = right_product.astype(jnp.bfloat16)
    own_rows = jnp.stack([second_field, third_field, right_product], axis=1)
    all_source, all_left, all_right = (
        lax.all_gather(source_slice, "tm", axis=0, tiled=True),
        lax.all_gather(noise_left, "tm", axis=0, tiled=True),
        lax.all_gather(noise_right, "tm", axis=0, tiled=True),
    )
    first_slice = lax.axis_index("tm") * slices
    slice_ids = jnp.arange(slices, dtype=jnp.int32)
    hit_mask = (all_source[None, :] == first_slice + slice_ids[:, None]).astype(jnp.bfloat16)
    pieces = jnp.einsum(
        "tj,jci,jdk->tcdik", hit_mask, all_left, all_right, preferred_element_type=jnp.float32
    )
    weights = jnp.stack(
        [pieces[:, 0, 0] - pieces[:, 1, 1], pieces[:, 0, 1] + pieces[:, 1, 0]], axis=1
    ).astype(jnp.bfloat16)

    def absorb(totals, block_cols, offset):
        tables = (
            pair_table(first_field, block_cols[:, 0]),
            pair_table(fourth_field, block_cols[:, 1]),
            pair_table(left_product, block_cols[:, 2]),
            noise_table(weights, block_cols[:, 2]),
        )
        target = slice_ids[:, None] + separations[None, :] - offset * slices
        select = (target[:, :, None] == slice_ids[None, None, :]).astype(jnp.float32)
        return tuple(
            (
                running + jnp.einsum("tks,tsc->tkc", select, table, precision=lax.Precision.HIGHEST)
                for running, table in zip(totals, tables)
            )
        )

    nsep_count = separations.shape[0]
    blank = jnp.zeros((slices, nsep_count, 2), jnp.float32)
    totals = (blank, blank, blank, blank)
    shipped = to_columns(own_rows)
    totals = absorb(totals, shipped, 0)
    moving = shipped
    for offset in range(1, 4):
        moving = shifted(moving, "tm", -1)
        totals = absorb(totals, moving, offset)
    first_sum, second_sum, cross_sum, noise_sum = lax.psum(totals, "mode")
    box_trace = jnp.stack(
        [
            first_sum[..., 0] * second_sum[..., 0] - first_sum[..., 1] * second_sum[..., 1],
            first_sum[..., 0] * second_sum[..., 1] + first_sum[..., 1] * second_sum[..., 0],
        ],
        axis=-1,
    )
    return (box_trace, cross_sum, noise_sum)


def solution(mesh):
    in_specs = (
        P(None, "tm", None, "mode", None),
        P(None, "tm", "mode"),
        P(),
        P(),
        P("tm"),
        P("tm", None, None),
        P("tm", None, "mode"),
    )
    out_specs = (P("tm", None, None), P("tm", None, None), P("tm", None, None))
    return jax.shard_map(
        on_device, mesh=mesh, in_specs=in_specs, out_specs=out_specs, check_vma=False
    )
```

profile of v0, /device:TPU:1, one launch (start us, length us, event | category | flops | bytes accessed | tf_op | source)
XLA Modules:
  0.0 1055.6 jit_solution(925177968763349768)
XLA Ops:
  29.9 64.9 %all-gather.11.cloned.1.call-done = bf16[1,2,2,1024,1024]{3,4,2,1,0:T(8,128)(2,1)} async-done(((bf16[1,2,2,256,1024]{3,4,2,1,0:T(8,128)(2,1)}), bf16[1,2,2,1024,1024]{3,4,2,1,0:T(8,128)(2,1)}) %all-gather.11.cloned.1.call-update) | async-done | bytes 8388624 | tf_op jit(solution)/shard_map/all_gather | solution.py:50
  104.6 29.1 %copy.204 = bf16[2,3,2,256,1024]{3,2,0,1,4:T(2,128)(2,1)} copy(bf16[2,3,2,256,1024]{3,4,2,0,1:T(8,128)(2,1)S(1)} %maximum_maximum_fusion) | data formatting | bytes 12582912 | tf_op jit(solution)/shard_map/stack | solution.py:56
  140.8 108.9 %all-reduce = s32[2048]{0:T(1024)S(1)} all-reduce(s32[2048]{0:T(1024)S(1)} %dynamic-update-slice), channel_id=1, replica_groups=mesh['tm'=32,'mode'=4] {'tm'}, use_global_device_ids=true, to_apply=%add | all-reduce | flops 2048 | bytes 16384
  249.9 14.1 %copy.341 = bf16[2,3,2,256,4,256]{3,4,2,5,0,1:T(4,128)(2,1)} copy(bf16[2,3,2,256,4,256]{3,2,0,1,5,4:T(2,128)(2,1)} %bitcast.11) | data formatting | bytes 12582912 | tf_op jit(solution)/shard_map/all_to_all | solution.py:32
  296.2 153.9 %all-gather.13.cloned.1.call-done = bf16[1,2,2,1024,1024]{3,4,2,1,0:T(8,128)(2,1)} async-done(((bf16[1,2,2,256,1024]{3,4,2,1,0:T(8,128)(2,1)}), bf16[1,2,2,1024,1024]{3,4,2,1,0:T(8,128)(2,1)}) %all-gather.13.cloned.1.call-update) | async-done | bytes 8388624 | tf_op jit(solution)/shard_map/all_gather | solution.py:49
  463.2 171.3 %all-gather.9.cloned.1.call-done = bf16[2048,2,1024]{2,0,1:T(8,128)(2,1)} async-done(((bf16[64,2,1024]{2,0,1:T(8,128)(2,1)}), bf16[2048,2,1024]{2,0,1:T(8,128)(2,1)}) %all-gather.9.cloned.1.call-update) | async-done | bytes 8388624 | tf_op jit(solution)/shard_map/all_gather | solution.py:59
  634.5 12.7 %fusion.16 = f32[2,2,2,1024,256]{3,4,1,0,2:T(8,128)S(1)} fusion(bf16[2048,2,1024]{2,0,1:T(8,128)(2,1)} %all-gather.9.cloned.1.call-done, f32[2048,2,256]{0,2,1:T(8,128)} %copy.270, f32[2048,2]{0,1:T(2,128)S(1)} %fusion.95), kind=kOutput, calls=%fused_computation.15 | convolution fusion | flops 8592031744 | bytes 20987904 | tf_op jit(solution)/shard_map/tj,jci,jdk->tcdik/dot_general | solution.py:65
  650.5 20.3 %convolution_bitcast_fusion.3 = f32[2,2,2,2]{2,3,0,1:T(2,128)S(1)} fusion(bf16[2,2,1024,256,1]{2,1,3,0,4:T(2,128)(2,1)S(1)} %bitcast.448, bf16[2,3,2,1024,256]{3,2,4,0,1:T(2,128)(2,1)S(1)} %bitcast.447), kind=kOutput, calls=%fused_computation.93 | convolution fusion | flops 8388608 | bytes 4194368 | tf_op jit(solution)/shard_map/tcik,sdik->tscd/dot_general | solution.py:25
  674.7 19.9 %fusion.55 = f32[2,2,2,2]{2,3,0,1:T(2,128)S(1)} fusion(bf16[2,2,256,1024]{3,1,2,0:T(2,128)(2,1)S(1)} %copy-done.4, bf16[2,3,2,1024,256]{3,2,4,0,1:T(2,128)(2,1)S(1)} %bitcast.447), kind=kOutput, calls=%fused_computation.78 | convolution fusion | flops 8388608 | bytes 4194368 | tf_op jit(solution)/shard_map/tcij,sdji->tscd/dot_general | solution.py:18
  695.1 21.8 %fusion.76 = f32[2,2,2,2]{2,3,0,1:T(2,128)S(1)} fusion(bf16[2,2,256,1024]{3,1,2,0:T(2,128)(2,1)S(1)} %copy-done.3, bf16[2,3,2,1024,256]{3,2,4,0,1:T(2,128)(2,1)} %all_to_all.16), kind=kOutput, calls=%fused_computation.85 | convolution fusion | flops 8388608 | bytes 4194368 | tf_op jit(solution)/shard_map/tcij,sdji->tscd/dot_general | solution.py:18
  717.2 22.5 %fusion.88 = f32[2,2,2,2]{2,3,0,1:T(2,128)S(1)} fusion(bf16[2,2,256,1024]{3,1,2,0:T(2,128)(2,1)} %copy.206, bf16[2,3,2,1024,256]{3,2,4,0,1:T(2,128)(2,1)} %all_to_all.16), kind=kOutput, calls=%fused_computation.89 | convolution fusion | flops 8388608 | bytes 4194368 | tf_op jit(solution)/shard_map/tcij,sdji->tscd/dot_general | solution.py:18
  740.5 22.7 %convolution_bitcast_fusion.2 = f32[2,2,2,2]{2,3,0,1:T(2,128)S(1)} fusion(bf16[2,2,1024,256,1]{2,1,3,0,4:T(2,128)(2,1)} %bitcast.449, bf16[2,3,2,1024,256]{3,2,4,0,1:T(2,128)(2,1)} %collective-permute-done), kind=kOutput, calls=%fused_computation.92 | convolution fusion | flops 8388608 | bytes 4194368 | tf_op jit(solution)/shard_map/tcik,sdik->tscd/dot_general | solution.py:25
  763.5 22.4 %fusion.58 = f32[2,2,2,2]{2,3,0,1:T(2,128)S(1)} fusion(bf16[2,2,256,1024]{3,1,2,0:T(2,128)(2,1)} %copy.249, bf16[2,3,2,1024,256]{3,2,4,0,1:T(2,128)(2,1)} %collective-permute-done), kind=kOutput, calls=%fused_computation.79 | convolution fusion | flops 8388608 | bytes 4194368 | tf_op jit(solution)/shard_map/tcij,sdji->tscd/dot_general | solution.py:18
  786.2 22.0 %fusion.73 = f32[2,2,2,2]{2,3,0,1:T(2,128)S(1)} fusion(bf16[2,2,256,1024]{3,1,2,0:T(2,128)(2,1)S(1)} %copy-done.3, bf16[2,3,2,1024,256]{3,2,4,0,1:T(2,128)(2,1)} %collective-permute-done), kind=kOutput, calls=%fused_computation.84 | convolution fusion | flops 8388608 | bytes 4194368 | tf_op jit(solution)/shard_map/tcij,sdji->tscd/dot_general | solution.py:18
  814.7 22.3 %fusion.85 = f32[2,2,2,2]{2,3,0,1:T(2,128)S(1)} fusion(bf16[2,2,256,1024]{3,1,2,0:T(2,128)(2,1)} %copy.206, bf16[2,3,2,1024,256]{3,2,4,0,1:T(2,128)(2,1)} %collective-permute-done), kind=kOutput, calls=%fused_computation.88 | convolution fusion | flops 8388608 | bytes 4194368 | tf_op jit(solution)/shard_map/tcij,sdji->tscd/dot_general | solution.py:18
  837.8 22.4 %convolution_bitcast_fusion.1 = f32[2,2,2,2]{2,3,0,1:T(2,128)S(1)} fusion(bf16[2,2,1024,256,1]{2,1,3,0,4:T(2,128)(2,1)} %bitcast.450, bf16[2,3,2,1024,256]{3,2,4,0,1:T(2,128)(2,1)} %collective-permute-done.1), kind=kOutput, calls=%fused_computation.91 | convolution fusion | flops 8388608 | bytes 4194368 | tf_op jit(solution)/shard_map/tcik,sdik->tscd/dot_general | solution.py:25
  860.5 22.5 %fusion.61 = f32[2,2,2,2]{2,3,0,1:T(2,128)S(1)} fusion(bf16[2,2,256,1024]{3,1,2,0:T(2,128)(2,1)} %copy.249, bf16[2,3,2,1024,256]{3,2,4,0,1:T(2,128)(2,1)} %collective-permute-done.1), kind=kOutput, calls=%fused_computation.80 | convolution fusion | flops 8388608 | bytes 4194368 | tf_op jit(solution)/shard_map/tcij,sdji->tscd/dot_general | solution.py:18
  883.2 22.0 %fusion.70 = f32[2,2,2,2]{2,3,0,1:T(2,128)S(1)} fusion(bf16[2,2,256,1024]{3,1,2,0:T(2,128)(2,1)S(1)} %copy-done.3, bf16[2,3,2,1024,256]{3,2,4,0,1:T(2,128)(2,1)} %collective-permute-done.1), kind=kOutput, calls=%fused_computation.83 | convolution fusion | flops 8388608 | bytes 4194368 | tf_op jit(solution)/shard_map/tcij,sdji->tscd/dot_general | solution.py:18
  905.6 22.4 %fusion.82 = f32[2,2,2,2]{2,3,0,1:T(2,128)S(1)} fusion(bf16[2,2,256,1024]{3,1,2,0:T(2,128)(2,1)} %copy.206, bf16[2,3,2,1024,256]{3,2,4,0,1:T(2,128)(2,1)} %collective-permute-done.1), kind=kOutput, calls=%fused_computation.87 | convolution fusion | flops 8388608 | bytes 4194368 | tf_op jit(solution)/shard_map/tcij,sdji->tscd/dot_general | solution.py:18
  928.8 18.5 %collective-permute-done.2 = bf16[2,3,2,1024,256]{3,2,4,0,1:T(2,128)(2,1)} collective-permute-done((bf16[2,3,2,1024,256]{3,2,4,0,1:T(2,128)(2,1)}, bf16[2,3,2,1024,256]{3,2,4,0,1:T(2,128)(2,1)}, u32[]{:S(2)}, u32[]{:S(2)}) %collective-permute-start.2) | collective-permute-done | bytes 6291488 | tf_op jit(solution)/shard_map/ppermute | solution.py:9
  947.4 22.5 %fusion.79 = f32[2,2,2,2]{2,3,0,1:T(2,128)S(1)} fusion(bf16[2,2,256,1024]{3,1,2,0:T(2,128)(2,1)} %copy.206, bf16[2,3,2,1024,256]{3,2,4,0,1:T(2,128)(2,1)} %collective-permute-done.2), kind=kOutput, calls=%fused_computation.86 | convolution fusion | flops 8388608 | bytes 4194368 | tf_op jit(solution)/shard_map/tcij,sdji->tscd/dot_general | solution.py:18
  970.0 22.0 %fusion.67 = f32[2,2,2,2]{2,3,0,1:T(2,128)S(1)} fusion(bf16[2,2,256,1024]{3,1,2,0:T(2,128)(2,1)S(1)} %copy-done.3, bf16[2,3,2,1024,256]{3,2,4,0,1:T(2,128)(2,1)} %collective-permute-done.2), kind=kOutput, calls=%fused_computation.82 | convolution fusion | flops 8388608 | bytes 4194368 | tf_op jit(solution)/shard_map/tcij,sdji->tscd/dot_general | solution.py:18
  992.2 22.4 %fusion.64 = f32[2,2,2,2]{2,3,0,1:T(2,128)S(1)} fusion(bf16[2,2,256,1024]{3,1,2,0:T(2,128)(2,1)} %copy.249, bf16[2,3,2,1024,256]{3,2,4,0,1:T(2,128)(2,1)} %collective-permute-done.2), kind=kOutput, calls=%fused_computation.81 | convolution fusion | flops 8388608 | bytes 4194368 | tf_op jit(solution)/shard_map/tcij,sdji->tscd/dot_general | solution.py:18
  1014.8 21.8 %convolution_bitcast_fusion = f32[2,2,2,2]{2,3,0,1:T(2,128)S(1)} fusion(bf16[2,2,1024,256,1]{2,1,3,0,4:T(2,128)(2,1)S(1)} %bitcast.451, bf16[2,3,2,1024,256]{3,2,4,0,1:T(2,128)(2,1)} %collective-permute-done.2), kind=kOutput, calls=%fused_computation.90 | convolution fusion | flops 8388608 | bytes 4194368 | tf_op jit(solution)/shard_map/tcik,sdik->tscd/dot_general | solution.py:25
  (140 shorter events, 110.1 us)
Async XLA Ops:
  7.2 87.6 %all-gather.11.cloned.1.call-start = ((), (), s32[]{:S(2)}) async-start(), calls=%async_computation.3 | async-start | bytes 10485760 | tf_op jit(solution)/shard_map/all_gather | solution.py:50
  13.8 6.2 copy-start.8
  23.0 4.5 copy-start.2
  27.5 1.6 copy-start.7
  27.5 259.3 %all-gather.7.cloned.1.call-start = ((), (), s32[]{:S(2)}) async-start(), calls=%async_computation.1 | async-start | bytes 2162688 | tf_op jit(solution)/shard_map/all_gather | solution.py:60
  28.3 421.7 %all-gather.13.cloned.1.call-start = ((), (), s32[]{:S(2)}) async-start(), calls=%async_computation.4 | async-start | bytes 10485760 | tf_op jit(solution)/shard_map/all_gather | solution.py:49
  29.0 605.5 %all-gather.9.cloned.1.call-start = ((), (), s32[]{:S(2)}) async-start(), calls=%async_computation.2 | async-start | bytes 8650752 | tf_op jit(solution)/shard_map/all_gather | solution.py:59
  102.3 1.6 copy-start.1
  133.7 5.6 copy-start.11
  133.7 6.9 copy-start.10
  133.7 116.2 %all-to-all-start = ((bf16[2,3,2,256,1024]{3,2,0,1,4:T(2,128)(2,1)}), bf16[2,3,2,256,1024]{3,2,0,1,4:T(2,128)(2,1)}, u32[]{:S(2)}, u32[]{:S(2)}) async-start(bf16[2,3,2,256,1024]{3,2,0,1,4:T(2,128)(2,1)} %copy.204), calls=%async_computation | async-start | bytes 12582912 | tf_op jit(solution)/shard_map/all_to_all | solution.py:32
  264.0 12.4 %copy-start.9 = (s32[3]{0:T(128)S(1)}, s32[3]{0:T(128)}, u32[]{:S(2)}) copy-start(s32[3]{0:T(128)} %param.10) | copy-start | bytes 40
  274.3 396.5 %collective-permute-start = (bf16[2,3,2,1024,256]{3,2,4,0,1:T(2,128)(2,1)}, bf16[2,3,2,1024,256]{3,2,4,0,1:T(2,128)(2,1)}, u32[]{:S(2)}, u32[]{:S(2)}) collective-permute-start(bf16[2,3,2,1024,256]{3,2,4,0,1:T(2,128)(2,1)} %all_to_all.16), channel_id=1, source_target_pairs={{0,124},{4,0},{8,4},{12,8},{16,12},{20,16},{24,20},{28,24},{32,28}... | collective-permute-start | bytes 18874376 | tf_op jit(solution)/shard_map/ppermute | solution.py:9
  276.4 6.4 copy-start
  647.5 2.7 slice-start
  647.9 2.6 slice-start.1
  650.2 20.5 %copy-start.5 = (bf16[2,2,1024,256]{2,1,3,0:T(2,128)(2,1)}, bf16[2,2,1024,256]{2,1,3,0:T(2,128)(2,1)S(1)}, u32[]{:S(2)}) copy-start(bf16[2,2,1024,256]{2,1,3,0:T(2,128)(2,1)S(1)} %copy.342) | copy-start | bytes 6291460
  650.5 24.2 %copy-start.4 = (bf16[2,2,256,1024]{3,1,2,0:T(2,128)(2,1)S(1)}, bf16[2,2,256,1024]{3,1,2,0:T(2,128)(2,1)}, u32[]{:S(2)}) copy-start(bf16[2,2,256,1024]{3,1,2,0:T(2,128)(2,1)} %copy.249) | copy-start | bytes 6291460
  670.8 24.4 %copy-start.3 = (bf16[2,2,256,1024]{3,1,2,0:T(2,128)(2,1)S(1)}, bf16[2,2,256,1024]{3,1,2,0:T(2,128)(2,1)}, u32[]{:S(2)}) copy-start(bf16[2,2,256,1024]{3,1,2,0:T(2,128)(2,1)} %copy.226) | copy-start | bytes 6291460
  670.8 137.7 %collective-permute-start.1 = (bf16[2,3,2,1024,256]{3,2,4,0,1:T(2,128)(2,1)}, bf16[2,3,2,1024,256]{3,2,4,0,1:T(2,128)(2,1)}, u32[]{:S(2)}, u32[]{:S(2)}) collective-permute-start(bf16[2,3,2,1024,256]{3,2,4,0,1:T(2,128)(2,1)} %collective-permute-done), channel_id=1, source_target_pairs={{0,124},{4,0},{8,4},{12,8},{16,12},{20,16},{24,20},{28,24},{32,28}... | collective-permute-start | bytes 18874376 | tf_op jit(solution)/shard_map/ppermute | solution.py:9
  808.5 138.9 %collective-permute-start.2 = (bf16[2,3,2,1024,256]{3,2,4,0,1:T(2,128)(2,1)}, bf16[2,3,2,1024,256]{3,2,4,0,1:T(2,128)(2,1)}, u32[]{:S(2)}, u32[]{:S(2)}) collective-permute-start(bf16[2,3,2,1024,256]{3,2,4,0,1:T(2,128)(2,1)} %collective-permute-done.1), channel_id=1, source_target_pairs={{0,124},{4,0},{8,4},{12,8},{16,12},{20,16},{24,20},{28,24},{32,28}... | collective-permute-start | bytes 18874376 | tf_op jit(solution)/shard_map/ppermute | solution.py:9
  992.2 22.6 %copy-start.6 = (bf16[2,2,1024,256]{2,1,3,0:T(2,128)(2,1)S(1)}, bf16[2,2,1024,256]{2,1,3,0:T(2,128)(2,1)}, u32[]{:S(2)}) copy-start(bf16[2,2,1024,256]{2,1,3,0:T(2,128)(2,1)} %copy-done.5) | copy-start | bytes 6291460
Sparse Core Ops, SparseCore 0:
  27.6 67.0 all-gather.10
  96.4 131.7 all-gather.6
  229.9 220.0 all-gather.12
  451.5 182.9 all-gather.8
where the time goes:
time: 1060 us
  waiting for transfers between devices  410 us (39%)
  matrix products  383 us (36%)
  blocking collectives  119 us (11%)
  local copies, waits for them, and re-layouts  90.1 us (8%)
  between operations  20 us (2%)
  starting transfers between devices  17.9 us (2%)
  other arithmetic  15.4 us (1%)
    dot_general x12, matrix products, pair_table(): jnp.einsum('tcij,sdji->tscd', rows_part, cols_part, preferred_element_typ...  265 us
    all_gather x1, waiting for transfers between devices, on_device(): lax.all_gather(noise_left, 'tm', axis=0, tiled=True)  171 us
    all_gather x1, waiting for transfers between devices, on_device(): lax.all_gather(first_field, 'mode', axis=2, tiled=True)  154 us
    unnamed x1, blocking collectives  109 us
    dot_general x4, matrix products, noise_table(): jnp.einsum('tcik,sdik->tscd', weights, cols_part, preferred_element_type=...  87.2 us
    all_gather x1, waiting for transfers between devices, on_device(): lax.all_gather(third_field, 'mode', axis=2, tiled=True)  64.9 us
    another operation x1, local copies, waits for them, and re-layouts, on_device(): own_rows = jnp.stack([second_field, third_field, right_product], axis=1)  29.1 us
    all_to_all x2, local copies, waits for them, and re-layouts, to_columns(): lax.all_to_all(rows_stack, 'mode', split_axis=4, concat_axis=3, tiled=True)  24.4 us
  transfers between devices with their start and end apart: 8, of which 4 were waited for; matrix products, arithmetic and copies ran while one was open for 35% of the time, Pallas kernels for 0%

commit v1 on v0

v1 whole, which is shorter than its diff:
```python
import jax
import jax.numpy as jnp
from jax import lax
from jax.experimental import pallas as pl
from jax.experimental.pallas import tpu as pltpu
from jax.sharding import PartitionSpec as P

MESH = pl.DeviceIdType.MESH
ANY = pl.ANY
PLANE = 8
PLANES = 4
BLK = 128
HALO = 6
SPAN = 16
VMEM_LIMIT = 50 * 1024 * 1024


def home(row, e):
    if e == 0:
        return 0, row % 4, row // 4
    if e == 4:
        return 1, row % 4, row // 4
    if e < 4:
        return 2 * e + row // 4, row % 4, 0
    col = (row + e) % 8
    return 2 * (8 - e) + col // 4, col % 4, 1


def place():
    tm = lax.axis_index("tm")
    mode = lax.axis_index("mode")
    return tm, mode


def greet(tm, mode):
    base = (tm // PLANE) * PLANE
    barrier = pltpu.get_barrier_semaphore()
    for index in range(PLANE):
        for other in range(4):

            @pl.when(jnp.logical_or(base + index != tm, mode != other))
            def _():
                pl.semaphore_signal(
                    barrier, inc=1, device_id=(base + index, other), device_id_type=MESH
                )

    for step in (PLANE, 3 * PLANE):
        pl.semaphore_signal(
            barrier, inc=1, device_id=((tm + step) % 32, mode), device_id_type=MESH
        )
    pl.semaphore_wait(barrier, 33)


def remote(src, dst, send, recv, device):
    return pltpu.make_async_remote_copy(
        src_ref=src, dst_ref=dst, send_sem=send, recv_sem=recv,
        device_id=device, device_id_type=MESH,
    )


def send_or_keep(src, dst, send, recv, device, tm, mode):
    here = jnp.logical_and(device[0] == tm, device[1] == mode)

    @pl.when(jnp.logical_not(here))
    def _():
        remote(src, dst, send, recv, device).start()

    @pl.when(here)
    def _():
        pltpu.make_async_copy(src, dst, recv).start()


def sent(src, dst, send, recv, device, tm, mode):
    here = jnp.logical_and(device[0] == tm, device[1] == mode)

    @pl.when(jnp.logical_not(here))
    def _():
        remote(src, dst, send, recv, device).wait_send()


def landed(ref, sem):
    pltpu.make_async_copy(ref, ref, sem).wait()


def spread_fields(
    fields, noise, whole, homes, hits,
    asm_send, asm_recv, fwd_send, fwd_recv, fld_send, fld_recv, halo_send, halo_recv,
    hit_send, hit_recv, ring_send, ring_recv, relay_send, relay_recv,
):
    tm, mode = place()
    plane, local = tm // PLANE, tm % PLANE
    base = plane * PLANE
    core = mode % 2
    flip = tm + 1 - 2 * (tm % 2)
    sibling = mode + 1 - 2 * core
    greet(tm, mode)

    def rows_of(block):
        return whole.at[:, :, pl.ds(pl.multiple_of(block * 256, 256), 256), :]

    assembly = [
        remote(fields.at[:, s], rows_of(mode), asm_send.at[s], asm_recv.at[mode // 2],
               (flip, 2 * s + core))
        for s in range(2)
    ]
    for copy in assembly:
        copy.start()

    hit_copies = []
    for a in range(2):
        for e in range(8):
            row = 2 * mode + a
            at, other, slot = home(row, e)
            hit_copies.append((
                noise.at[a], hits.at[slot, plane, local], hit_send.at[a, e],
                hit_recv.at[slot, local], (base + at, other),
            ))
    for copy in hit_copies:
        send_or_keep(*copy, tm, mode)

    field_copies = []
    for s in range(2):
        for a in range(2):
            for e in range(8):
                row = 2 * mode + a
                col = (row + e) % 8
                at, other, slot = home(row, e)
                field_copies.append((
                    fields.at[:, s, :, pl.ds(a * BLK, BLK),
                              pl.ds(pl.multiple_of(col * BLK, BLK), BLK)],
                    homes.at[slot, 2 * local + s], fld_send.at[s, a, e],
                    fld_recv.at[slot, 2 * local + s], (base + at, other),
                ))
    for copy in field_copies:
        send_or_keep(*copy, tm, mode)

    forwards = []
    for h in range(2):
        block = rows_of(2 * h + core)
        landed(block, asm_recv.at[h])
        forwards.append(
            remote(block, block, fwd_send.at[h], fwd_recv.at[h], (tm, sibling))
        )
        forwards[-1].start()

    right = ((tm + PLANE) % 32, mode)
    left = ((tm + 3 * PLANE) % 32, mode)
    for slot in range(2):
        for q in range(PLANE):
            landed(hits.at[slot, plane, q], hit_recv.at[slot, q])
    own = hits.at[:, plane]
    ring = [
        remote(own, own, ring_send.at[0], ring_recv.at[0], right),
        remote(own, own, ring_send.at[1], ring_recv.at[1], left),
    ]
    for copy in ring:
        copy.start()

    halos = []
    for slot in range(2):
        for t in range(HALO):
            landed(homes.at[slot, t], fld_recv.at[slot, t])
        halos.append(remote(
            homes.at[slot, pl.ds(0, HALO)], homes.at[slot, pl.ds(SPAN, HALO)],
            halo_send.at[slot], halo_recv.at[slot], left,
        ))
        halos[-1].start()

    before = (plane + 3) % PLANES
    after = (plane + 1) % PLANES
    opposite = (plane + 2) % PLANES
    landed(hits.at[:, before], ring_recv.at[0])
    relays = [remote(hits.at[0, before], hits.at[0, before], relay_send.at[0],
                     relay_recv.at[0], right)]
    relays[0].start()
    landed(hits.at[:, after], ring_recv.at[1])
    relays.append(remote(hits.at[1, after], hits.at[1, after], relay_send.at[1],
                         relay_recv.at[1], left))
    relays[1].start()

    for slot in range(2):
        for t in range(HALO, SPAN):
            landed(homes.at[slot, t], fld_recv.at[slot, t])
    for h in range(2):
        landed(rows_of(2 * h + 1 - core), fwd_recv.at[h])
    for slot in range(2):
        landed(homes.at[slot, pl.ds(SPAN, HALO)], halo_recv.at[slot])
        landed(hits.at[slot, opposite], relay_recv.at[slot])
    for copy in assembly + forwards + ring + halos + relays:
        copy.wait_send()
    for copy in hit_copies + field_copies:
        sent(*copy, tm, mode)


def multiply(mom, whole, out):
    core = lax.axis_index("mode") % 2
    start = pl.multiple_of(core * 512, 512)
    m1, m2, m3, m4 = (mom[i] for i in range(4))
    f32 = jnp.float32

    def cdot(ar, ai, br, bi):
        def dot(a, b):
            return jnp.dot(a, b, preferred_element_type=f32)

        return dot(ar, br) - dot(ai, bi), dot(ar, bi) + dot(ai, br)

    @pl.loop(0, 4)
    def _(step):
        pair, half = step // 2, step % 2
        cols = pl.ds(pl.multiple_of(start + pair * 256, 256), 256)
        rows = pl.ds(pl.multiple_of(half * 512, 512), 512)
        parts = cdot(whole[m4, 0, rows, :], whole[m4, 1, rows, :],
                     whole[m1, 0, :, cols], whole[m1, 1, :, cols])
        for c in range(2):
            for a in range(2):
                for b in range(4):
                    piece = parts[c][b * BLK:(b + 1) * BLK, a * BLK:(a + 1) * BLK]
                    out[2 * pair + a, 4 * half + b, c] = piece.T.astype(jnp.bfloat16)

    @pl.loop(0, 4)
    def _(pair):
        cols = pl.ds(pl.multiple_of(pair * 256, 256), 256)
        rows = pl.ds(start, 512)
        parts = cdot(whole[m2, 0, rows, :], whole[m2, 1, rows, :],
                     whole[m3, 0, :, cols], whole[m3, 1, :, cols])
        for c in range(2):
            for a in range(4):
                for b in range(2):
                    piece = parts[c][a * BLK:(a + 1) * BLK, b * BLK:(b + 1) * BLK]
                    out[a, 2 * pair + b, 2 + c] = piece.astype(jnp.bfloat16)


def spread_products(products, homes, send, recv, halo_send, halo_recv):
    tm, mode = place()
    base = (tm // PLANE) * PLANE
    core = mode % 2
    flip = tm + 1 - 2 * (tm % 2)
    when = 2 * (flip % PLANE) + mode // 2
    left = ((tm + 3 * PLANE) % 32, mode)
    greet(tm, mode)
    copies = []
    for e in range(8):
        for i in range(4):
            row = 4 * core + i
            col = (row + e) % 8
            at, other, slot = home(row, e)
            copies.append((
                products.at[i, col], homes.at[slot, when], send.at[i, e],
                recv.at[slot, when], (base + at, other),
            ))
    for copy in copies:
        send_or_keep(*copy, tm, mode)
    halos = []
    for slot in range(2):
        for t in range(HALO):
            landed(homes.at[slot, t], recv.at[slot, t])
        halos.append(remote(
            homes.at[slot, pl.ds(0, HALO), pl.ds(2, 2)],
            homes.at[slot, pl.ds(SPAN, HALO), pl.ds(2, 2)],
            halo_send.at[slot], halo_recv.at[slot], left,
        ))
        halos[-1].start()
    for slot in range(2):
        for t in range(HALO, SPAN):
            landed(homes.at[slot, t], recv.at[slot, t])
    for slot in range(2):
        landed(homes.at[slot, pl.ds(SPAN, HALO), pl.ds(2, 2)], halo_recv.at[slot])
    for copy in halos:
        copy.wait_send()
    for copy in copies:
        sent(*copy, tm, mode)


def traces(mom, seps, fields, products, hits, out, left_t, source, sums):
    f32 = jnp.float32
    tm = lax.axis_index("tm")
    plane, local = tm // PLANE, tm % PLANE
    diagonal = local == 0
    m1, m2, m3, m4 = (mom[i] for i in range(4))

    for role in range(2):
        for c in range(2):
            @pl.loop(0, 16)
            def _(part):
                block = hits[role, part // 4, pl.ds(2 * (part % 4), 2), c].reshape(BLK, BLK)
                left_t[role, pl.ds(c * BLK, BLK), pl.ds(pl.multiple_of(part * BLK, BLK), BLK)] = block.T

    @pl.loop(0, 16)
    def _(part):
        block = hits[0, part // 4, pl.ds(2 * (part % 4), 2), 4].reshape(BLK, BLK)
        source[:, pl.ds(pl.multiple_of(part * BLK, BLK), BLK)] = block.T[:16]

    def fold(value):
        return jnp.sum(value, axis=0, keepdims=True)

    @pl.loop(0, SPAN)
    def _(t):
        stamp = (plane * SPAN + t).astype(f32)
        chosen = (source[:1, :].astype(f32) == stamp).astype(f32).astype(jnp.bfloat16)
        totals = [[jnp.zeros((1, BLK), f32) for _ in range(8)] for _ in range(3)]
        for slot in range(2):
            mate = jnp.where(diagonal, slot, 1 - slot)
            right = jnp.concatenate(
                [hits[mate, :, :, 2 + c].reshape(2048, BLK) for c in range(2)], axis=1
            )
            pieces = jnp.dot(left_t[slot] * chosen, right, preferred_element_type=f32)
            w_re = pieces[:BLK, :BLK] - pieces[BLK:, BLK:]
            w_im = pieces[:BLK, BLK:] + pieces[BLK:, :BLK]
            p1 = [fields[slot, t, m1, c].astype(f32).T for c in range(2)]
            p4 = [fields[slot, t, m4, c].astype(f32).T for c in range(2)]
            rt = [products[slot, t, c].astype(f32) for c in range(2)]
            for k in range(3):
                u = t + seps[k]
                p2 = [fields[mate, u, m2, c].astype(f32) for c in range(2)]
                p3 = [fields[mate, u, m3, c].astype(f32) for c in range(2)]
                s = [products[slot, u, 2 + c].astype(f32) for c in range(2)]
                for at, (one, two) in enumerate(
                    ((p1, p2), (p4, p3), (rt, s), ((w_re, w_im), s))
                ):
                    totals[k][2 * at] += fold(one[0] * two[0] - one[1] * two[1])
                    totals[k][2 * at + 1] += fold(one[0] * two[1] + one[1] * two[0])
        for k in range(3):
            sums[3 * t + k] = jnp.concatenate(totals[k], axis=0)

    out[...] = jnp.sum(sums[...], axis=-1)


def params(ident=None):
    if ident is None:
        return pltpu.CompilerParams(vmem_limit_bytes=VMEM_LIMIT)
    return pltpu.CompilerParams(collective_id=ident, has_side_effects=True)


def on_device(field_codes, scales, mom_index, separations, source_slice, noise_left, noise_right):
    tm = lax.axis_index("tm")
    mode = lax.axis_index("mode")
    bf16, f32 = jnp.bfloat16, jnp.float32
    dma = pltpu.SemaphoreType.DMA
    fields = (field_codes.astype(f32) * scales[:, :, None, :, None]).astype(bf16)
    mine = lax.dynamic_slice_in_dim(noise_left, mode * 256, 256, axis=2)
    noise = jnp.concatenate(
        [mine, noise_right, jnp.broadcast_to(source_slice.astype(bf16)[:, None, None], (64, 1, 256))],
        axis=1,
    )
    noise = noise.reshape(64, 5, 2, BLK).transpose(2, 1, 0, 3)

    any_spec = pl.BlockSpec(memory_space=ANY)
    smem = pl.BlockSpec(memory_space=pltpu.SMEM)
    vmem = pl.BlockSpec(memory_space=pltpu.VMEM)
    whole, field_homes, hits = pl.pallas_call(
        spread_fields,
        out_shape=(
            jax.ShapeDtypeStruct((2, 2, 1024, 1024), bf16),
            jax.ShapeDtypeStruct((2, SPAN + HALO, 2, 2, BLK, BLK), bf16),
            jax.ShapeDtypeStruct((2, PLANES, PLANE, 5, 64, BLK), bf16),
        ),
        in_specs=[any_spec] * 2,
        out_specs=[any_spec] * 3,
        scratch_shapes=[
            dma((2,)), dma((2,)), dma((2,)), dma((2,)), dma((2, 2, 8)), dma((2, SPAN)),
            dma((2,)), dma((2,)), dma((2, 8)), dma((2, PLANE)), dma((2,)), dma((2,)),
            dma((2,)), dma((2,)),
        ],
        compiler_params=params(0),
        name="spread_fields",
    )(fields, noise)
    products = pl.pallas_call(
        multiply,
        out_shape=jax.ShapeDtypeStruct((4, 8, 4, BLK, BLK), bf16),
        in_specs=[smem, vmem],
        out_specs=vmem,
        compiler_params=params(),
        name="multiply",
    )(mom_index, whole)
    product_homes = pl.pallas_call(
        spread_products,
        out_shape=jax.ShapeDtypeStruct((2, SPAN + HALO, 4, BLK, BLK), bf16),
        in_specs=[any_spec],
        out_specs=any_spec,
        scratch_shapes=[dma((4, 8)), dma((2, SPAN)), dma((2,)), dma((2,))],
        compiler_params=params(1),
        name="spread_products",
    )(products)
    part = pl.pallas_call(
        traces,
        out_shape=jax.ShapeDtypeStruct((3 * SPAN, 8), f32),
        in_specs=[smem, smem, vmem, vmem, vmem],
        out_specs=vmem,
        scratch_shapes=[
            pltpu.VMEM((2, 2 * BLK, 2048), bf16),
            pltpu.VMEM((16, 2048), bf16),
            pltpu.VMEM((3 * SPAN, 8, BLK), f32),
        ],
        compiler_params=params(),
        name="traces",
    )(mom_index, separations, field_homes, product_homes, hits)

    table = jnp.zeros((64, 3, 8), f32)
    table = lax.dynamic_update_slice(
        table, part.reshape(SPAN, 3, 8), ((tm // PLANE) * SPAN, 0, 0)
    )
    total = lax.psum(table, ("tm", "mode"))
    mine = lax.dynamic_slice_in_dim(total, 2 * tm, 2, axis=0)
    box = jnp.stack(
        [
            mine[..., 0] * mine[..., 2] - mine[..., 1] * mine[..., 3],
            mine[..., 0] * mine[..., 3] + mine[..., 1] * mine[..., 2],
        ],
        axis=-1,
    )
    return box, mine[..., 4:6], mine[..., 6:8]


def solution(mesh):
    in_specs = (
        P(None, "tm", None, "mode", None),
        P(None, "tm", "mode"),
        P(),
        P(),
        P("tm"),
        P("tm", None, None),
        P("tm", None, "mode"),
    )
    out_specs = (P("tm", None, None), P("tm", None, None), P("tm", None, None))
    return jax.shard_map(
        on_device, mesh=mesh, in_specs=in_specs, out_specs=out_specs, check_vma=False
    )
```

time: 1060 us -> 396 us (0.37)
  waiting for transfers between devices: 410 us -> 0 us
  matrix products: 383 us -> 0 us
  Pallas kernels: 0 us -> 302 us
  local copies, waits for them, and re-layouts: 90.1 us -> 2.14 us
  blocking collectives: 119 us -> 83.6 us
  between operations: 20 us -> 0.75 us
  starting transfers between devices: 17.9 us -> 0 us
    all_gather x4 -> x0, waiting for transfers between devices: 390 us -> none  [the longest x1 171 us: on_device(): lax.all_gather(noise_left, 'tm', axis=0, tiled=True)]
    dot_general x35 -> x0, matrix products: 383 us -> none  [the longest x12 265 us: pair_table(): jnp.einsum('tcij,sdji->tscd', rows_part, cols_part, preferred_element_typ...]
    pallas_call x0 -> x4, Pallas kernels: none -> 302 us  [the longest x1 164 us: on_device(): pl.pallas_call(spread_fields, out_shape=(jax.ShapeDtypeStruct((2, 2, 1024...]
    unnamed x1 -> x0, blocking collectives: 109 us -> none
    psum x1, blocking collectives: 10.5 us -> 83.6 us  [on_device(): total = lax.psum(table, ('tm', 'mode'))]
    another operation x4 -> x0, local copies, waits for them, and re-layouts: 40.8 us -> none  [the longest x1 29.1 us: on_device(): own_rows = jnp.stack([second_field, third_field, right_product], axis=1)]
    all_to_all x2 -> x0, local copies, waits for them, and re-layouts: 24.4 us -> none  [to_columns(): lax.all_to_all(rows_stack, 'mode', split_axis=4, concat_axis=3, tiled=True)]
    ppermute x3 -> x0, waiting for transfers between devices: 18.5 us -> none  [shifted(): lax.ppermute(x, axis, [(i, (i + by) % devices) for i in range(devices)])]
  transfers between devices with their start and end apart: 8 -> 0, of which waited for: 4 -> 0; matrix products, arithmetic and copies ran while one was open for 35% -> 0% of each run, Pallas kernels for 0% -> 0%
where the time goes in v1:
time: 396 us
  Pallas kernels  302 us (76%)
  blocking collectives  83.6 us (21%)
  other arithmetic  7.28 us (2%)
    pallas_call x1, Pallas kernels, on_device(): pl.pallas_call(spread_fields, out_shape=(jax.ShapeDtypeStruct((2, 2, 1024...  164 us
    pallas_call x1, Pallas kernels, on_device(): pl.pallas_call(spread_products, out_shape=jax.ShapeDtypeStruct((2, SPAN +...  92.8 us
    psum x1, blocking collectives, on_device(): total = lax.psum(table, ('tm', 'mode'))  83.6 us
    pallas_call x1, Pallas kernels, on_device(): pl.pallas_call(traces, out_shape=jax.ShapeDtypeStruct((3 * SPAN, 8), f32)...  29.3 us
    pallas_call x1, Pallas kernels, on_device(): pl.pallas_call(multiply, out_shape=jax.ShapeDtypeStruct((4, 8, 4, BLK, BL...  16.2 us

profile of v1, /device:TPU:1, one launch (start us, length us, event | category | flops | bytes accessed | tf_op | source)
XLA Modules:
  0.0 396.2 jit_solution(18382216766206500747)
XLA Ops:
  0.6 0.0 copy-start
  0.7 0.9 copy-done
  1.6 0.7 convert_element_type.11
  2.3 0.1 broadcast_in_dim.5
  2.4 1.1 pad_maximum_fusion
  3.5 0.1 reshape.18
  3.6 0.7 copy.17
  4.3 0.0 copy-start.1
  4.3 4.9 %multiply_convert_fusion.fields = bf16[2,2,2,256,1024]{4,3,2,1,0:T(8,128)(2,1)} fusion(bf16[2,2,2,256,1024]{4,3,2,1,0:T(8,128)(2,1)} %param.7, f32[2,2,256]{2,1,0:T(2,128)} %param.8), kind=kLoop, calls=%fused_computation | loop fusion | flops 6291456 | bytes 8392704 | tf_op jit(solution)/shard_map/convert_element_type | solution.py:339
  9.3 164.1 %spread_fields.1 = (bf16[2,2,1024,1024]{3,2,1,0:T(8,128)(2,1)}, bf16[2,22,2,2,128,128]{5,4,3,2,1,0:T(8,128)(2,1)}, bf16[2,4,8,5,64,128]{5,4,3,2,1,0:T(8,128)(2,1)}) custom-call(bf16[2,2,2,256,1024]{4,3,2,1,0:T(8,128)(2,1)} %multiply_convert_fusion.fields, bf16[2,5,64,128]{3,2,1,0:T(8,128)(2,1)} %bitcast.3), custom_call_target="tpu_custom_call" | custom-call | tf_op jit(solution)/shard_map/spread_fields/pallas_call | solution.py:350
  173.3 0.0 copy-done.1
  173.3 16.2 %multiply.1.products = bf16[4,8,4,128,128]{4,3,2,1,0:T(8,128)(2,1)} custom-call(s32[4]{0:T(128)S(1)} %copy-done.1, bf16[2,2,1024,1024]{3,2,1,0:T(8,128)(2,1)} %get-tuple-element.7.whole), custom_call_target="tpu_custom_call" | custom-call | tf_op jit(solution)/shard_map/multiply/pallas_call | solution.py:367
  189.5 0.0 copy-start.2
  189.5 92.8 %spread_products.1.products = bf16[2,22,4,128,128]{4,3,2,1,0:T(8,128)(2,1)} custom-call(bf16[4,8,4,128,128]{4,3,2,1,0:T(8,128)(2,1)} %multiply.1.products), custom_call_target="tpu_custom_call" | custom-call | tf_op jit(solution)/shard_map/spread_products/pallas_call | solution.py:375
  282.4 0.0 copy-done.2
  282.4 29.3 %traces.1 = f32[48,8]{1,0:T(8,128)S(1)} custom-call(s32[4]{0:T(128)S(1)} %copy-done.1, s32[3]{0:T(128)S(1)} %copy-done.2, bf16[2,22,2,2,128,128]{5,4,3,2,1,0:T(8,128)(2,1)} %get-tuple-element.6.fields, bf16[2,22,4,128,128]{4,3,2,1,0:T(8,128)(2,1)} %spread_products.1.products, bf16[2,4,8,5,64,128]{5,4,3,2,1,0:T(8,128)(2,1)} %get-tuple-element.8.hits), custom_call_target="tpu_custom_call" | custom-call | tf_op jit(solution)/shard_map/traces/pallas_call | solution.py:384
  311.7 0.2 copy.13
  311.9 83.6 %psum.7 = f32[64,3,8]{1,2,0:T(8,128)S(1)} all-reduce(f32[64,3,8]{1,2,0:T(8,128)S(1)} %constant_dynamic-update-slice_fusion), channel_id=1, replica_groups=mesh['tm'=32,'mode'=4] {'tm','mode'}, use_global_device_ids=true, to_apply=%region_0.1 | all-reduce | flops 1536 | bytes 12288 | tf_op jit(solution)/shard_map/psum | solution.py:402
  395.6 0.6 constant_dynamic-slice_fusion.5
  (5 shorter events, 0.1 us)
Async XLA Ops:
  0.6 1.0 copy-start
  4.3 169.0 %copy-start.1 = (s32[4]{0:T(128)S(1)}, s32[4]{0:T(128)}, u32[]{:S(2)}) copy-start(s32[4]{0:T(128)} %mom.3) | copy-start | bytes 52
  189.5 92.8 %copy-start.2 = (s32[3]{0:T(128)S(1)}, s32[3]{0:T(128)}, u32[]{:S(2)}) copy-start(s32[3]{0:T(128)} %seps.1) | copy-start | bytes 40

commit v2 on v1

v2 whole, which is shorter than its diff:
```python
import jax
import jax.numpy as jnp
from jax import lax
from jax.experimental import pallas as pl
from jax.experimental.pallas import tpu as pltpu
from jax.sharding import PartitionSpec as P

MESH = pl.DeviceIdType.MESH
ANY = pl.ANY
BLK = 128
SPAN = 16
VMEM_LIMIT = 50 * 1024 * 1024


def home(i, half, e, same):
    if same:
        if e == 0:
            unit, slot = i % 2, i // 2
        elif e == 1:
            unit, slot = 4 + i, 0
        elif e == 2:
            unit, slot = 2 + i % 2, i // 2
        else:
            unit, slot = 4 + (i + 3) % 4, 1
        return unit // 2, 0, 2 * half + unit % 2, slot, 4 * half + (i + e) % 4
    return i + half * (e - i), 1, e + half * (i - e), half, 4 * (1 - half) + e


class Place:
    def __init__(self):
        self.tm = lax.axis_index("tm")
        self.mode = lax.axis_index("mode")
        self.x, self.z, self.lo = self.tm // 8, (self.tm // 2) % 4, self.tm % 2
        self.hi, self.core = self.mode // 2, self.mode % 2
        self.right = ((self.tm + 8) % 32, self.mode)
        self.left = ((self.tm + 24) % 32, self.mode)

    def at(self, z, lo, hi, core):
        return (8 * self.x + 2 * z + lo, 2 * hi + core)

    def is_here(self, device):
        return jnp.logical_and(device[0] == self.tm, device[1] == self.mode)


def greet(place, along_x):
    barrier = pltpu.get_barrier_semaphore()

    def signal(device):
        pl.semaphore_signal(barrier, inc=1, device_id=device, device_id_type=MESH)

    for core in range(2):
        for z in range(4):

            @pl.when(jnp.logical_or(place.z != z, place.core != core))
            def _():
                signal(place.at(z, place.lo, place.hi, core))

        for y in range(4):

            @pl.when(jnp.logical_or(place.lo != y // 2, place.hi != y % 2))
            def _():
                signal(place.at(place.z, y // 2, y % 2, core))

    if along_x:
        signal(place.right)
        signal(place.left)
    pl.semaphore_wait(barrier, 15 if along_x else 13)


def remote(src, dst, send, recv, device):
    return pltpu.make_async_remote_copy(
        src_ref=src, dst_ref=dst, send_sem=send, recv_sem=recv,
        device_id=device, device_id_type=MESH,
    )


def send_or_keep(place, src, dst, send, recv, device):
    here = place.is_here(device)

    @pl.when(jnp.logical_not(here))
    def _():
        remote(src, dst, send, recv, device).start()

    @pl.when(here)
    def _():
        pltpu.make_async_copy(src, dst, recv).start()


def sent(place, src, dst, send, recv, device):
    @pl.when(jnp.logical_not(place.is_here(device)))
    def _():
        remote(src, dst, send, recv, device).wait_send()


def landed(ref, sem):
    pltpu.make_async_copy(ref, ref, sem).wait()


def spread_fields(
    fields, noise, whole, homes, hits, mid, mid_hits,
    asm_send, asm_recv, fwd_send, fwd_recv, z_send, z_recv, y_send, y_recv,
    hit_z_send, hit_z_recv, hit_y_send, hit_y_recv,
):
    me = Place()
    flip = me.tm + 1 - 2 * me.lo
    greet(me, False)

    def rows_of(block):
        return whole.at[:, :, pl.ds(pl.multiple_of(block * 256, 256), 256), :]

    assembly = [
        remote(fields.at[s], rows_of(me.mode), asm_send.at[s], asm_recv.at[me.hi],
               (flip, 2 * s + me.core))
        for s in range(2)
    ]
    for copy in assembly:
        copy.start()

    along_z = []
    for a in range(2):
        for same in (False, True):
            for e in range(4):
                z, lo, mode, slot, col = home(2 * me.core + a, me.hi, e, same)
                group = slot if same else 2 + mode // 2
                device = me.at(z, me.lo, me.hi, mode % 2)
                index = (a, int(same), e)
                along_z.append((noise.at[a], mid_hits.at[group, me.z],
                                hit_z_send.at[index], hit_z_recv.at[group, me.z], device))
                along_z.append((
                    fields.at[:, :, :, pl.ds(a * BLK, BLK),
                              pl.ds(pl.multiple_of(col * BLK, BLK), BLK)],
                    mid.at[group, me.z], z_send.at[index], z_recv.at[group, me.z], device,
                ))
    for copy in along_z[0::2] + along_z[1::2]:
        send_or_keep(me, *copy)

    forwards = []
    for h in range(2):
        block = rows_of(2 * h + me.core)
        landed(block, asm_recv.at[h])
        forwards.append(remote(block, block, fwd_send.at[h], fwd_recv.at[h],
                               (me.tm, me.mode + 1 - 2 * me.core)))
        forwards[-1].start()

    along_y = []
    for source in range(4):
        for group in range(4):
            if group < 2:
                slot, device = group, me.at(me.z, 0, me.hi, me.core)
            else:
                slot, device = me.hi, me.at(me.z, 1, group - 2, me.core)
            landed(mid_hits.at[group, source], hit_z_recv.at[group, source])
            along_y.append((
                mid_hits.at[group, source], hits.at[slot, source, me.lo],
                hit_y_send.at[group, source], hit_y_recv.at[slot, source, me.lo], device,
            ))
            send_or_keep(me, *along_y[-1])
            landed(mid.at[group, source], z_recv.at[group, source])
            along_y.append((
                mid.at[group, source], homes.at[slot, source, pl.ds(2 * me.lo, 2)],
                y_send.at[group, source], y_recv.at[slot, source, me.lo], device,
            ))
            send_or_keep(me, *along_y[-1])

    for slot in range(2):
        for z in range(4):
            for lo in range(2):
                landed(hits.at[slot, z, lo], hit_y_recv.at[slot, z, lo])
                landed(homes.at[slot, z, pl.ds(2 * lo, 2)], y_recv.at[slot, z, lo])
    for h in range(2):
        landed(rows_of(2 * h + 1 - me.core), fwd_recv.at[h])
    for copy in assembly + forwards:
        copy.wait_send()
    for copy in along_z + along_y:
        sent(me, *copy)


def multiply(mom, whole, out):
    core = lax.axis_index("mode") % 2
    start = pl.multiple_of(core * 512, 512)
    m1, m2, m3, m4 = (mom[i] for i in range(4))
    f32 = jnp.float32

    def cdot(ar, ai, br, bi):
        def dot(a, b):
            return jnp.dot(a, b, preferred_element_type=f32)

        return dot(ar, br) - dot(ai, bi), dot(ar, bi) + dot(ai, br)

    @pl.loop(0, 4)
    def _(step):
        pair, half = step // 2, step % 2
        cols = pl.ds(pl.multiple_of(start + pair * 256, 256), 256)
        rows = pl.ds(pl.multiple_of(half * 512, 512), 512)
        parts = cdot(whole[m4, 0, rows, :], whole[m4, 1, rows, :],
                     whole[m1, 0, :, cols], whole[m1, 1, :, cols])
        for c in range(2):
            for a in range(2):
                for b in range(4):
                    piece = parts[c][b * BLK:(b + 1) * BLK, a * BLK:(a + 1) * BLK]
                    out[2 * pair + a, 4 * half + b, 2 + c] = piece.T.astype(jnp.bfloat16)

    @pl.loop(0, 4)
    def _(pair):
        cols = pl.ds(pl.multiple_of(pair * 256, 256), 256)
        rows = pl.ds(start, 512)
        parts = cdot(whole[m2, 0, rows, :], whole[m2, 1, rows, :],
                     whole[m3, 0, :, cols], whole[m3, 1, :, cols])
        for c in range(2):
            for a in range(4):
                for b in range(2):
                    piece = parts[c][a * BLK:(a + 1) * BLK, b * BLK:(b + 1) * BLK]
                    out[a, 2 * pair + b, c] = piece.astype(jnp.bfloat16)


def spread_products(
    products, fields, noise, homes, field_homes, hits, mid,
    send1, recv1, send2, recv2, halo_send, halo_recv, field_send, field_recv,
    ring_send, ring_recv, relay_send, relay_recv, keep,
):
    me = Place()
    greet(me, True)
    when = 2 * (1 - me.lo) + me.hi

    ring = []
    for slot in range(2):
        ring.append(remote(noise.at[slot], hits.at[slot, me.x], ring_send.at[0, slot],
                           ring_recv.at[0, slot], me.right))
        ring.append(remote(noise.at[1 - slot], hits.at[1 - slot, me.x], ring_send.at[1, 1 - slot],
                           ring_recv.at[1, 1 - slot], me.left))
    for copy in ring:
        copy.start()
    kept = []
    for slot in range(2):
        kept.append(pltpu.make_async_copy(noise.at[slot], hits.at[slot, me.x], keep.at[0, slot]))
        kept.append(pltpu.make_async_copy(fields.at[slot], field_homes.at[slot, pl.ds(0, 4)],
                                          keep.at[1, slot]))
    for copy in kept:
        copy.start()

    first = []
    for p in range(2):
        for i in range(4):
            for same in (False, True):
                for e in range(4):
                    z, lo, mode, slot, col = home(i, me.core, e, same)
                    hi, core = mode // 2, mode % 2

                    def either(one, two):
                        return one + slot * (two - one)

                    device = me.at(either(me.z, z), either(lo, me.lo), either(hi, me.hi), core)
                    at = (p, slot, either(z, 2 * lo + hi), either(when, me.z))
                    first.append((
                        products.at[i, col, pl.ds(2 * p, 2)], mid.at[at],
                        send1.at[p, i, int(same), e], recv1.at[at], device,
                    ))
    for copy in first:
        send_or_keep(me, *copy)

    halos = []
    for slot in range(2):
        halos.append(remote(fields.at[slot, 0], field_homes.at[slot, 4],
                            field_send.at[slot, 0], field_recv.at[slot, 0], me.left))
        halos.append(remote(fields.at[slot, 1, pl.ds(0, 2)], field_homes.at[slot, 5, pl.ds(0, 2)],
                            field_send.at[slot, 1], field_recv.at[slot, 1], me.left))
    for copy in halos:
        copy.start()

    before, after, opposite = (me.x + 3) % 4, (me.x + 1) % 4, (me.x + 2) % 4
    second = []
    relays = []

    def pass_on(p):
        for j in range(4):
            for k in range(4):
                landed(mid.at[p, 0, k, j], recv1.at[p, 0, k, j])
                second.append((
                    mid.at[p, 0, k, j], homes.at[0, me.z, j, pl.ds(2 * p, 2)],
                    send2.at[p, 0, k, j], recv2.at[p, 0, me.z, j],
                    me.at(k, me.lo, me.hi, me.core),
                ))
                send_or_keep(me, *second[-1])
                landed(mid.at[p, 1, k, j], recv1.at[p, 1, k, j])
                second.append((
                    mid.at[p, 1, k, j], homes.at[1, j, when, pl.ds(2 * p, 2)],
                    send2.at[p, 1, k, j], recv2.at[p, 1, j, when],
                    me.at(me.z, k // 2, k % 2, me.core),
                ))
                send_or_keep(me, *second[-1])

    def arrived(p, slot, z, t):
        landed(homes.at[slot, z, t, pl.ds(2 * p, 2)], recv2.at[p, slot, z, t])

    pass_on(0)
    landed(hits.at[0, before], ring_recv.at[0, 0])
    relays.append(remote(hits.at[0, before], hits.at[0, before], relay_send.at[0],
                         relay_recv.at[0], me.right))
    relays[-1].start()
    landed(hits.at[1, after], ring_recv.at[1, 1])
    relays.append(remote(hits.at[1, after], hits.at[1, after], relay_send.at[1],
                         relay_recv.at[1], me.left))
    relays[-1].start()
    for slot in range(2):
        for t in range(6):
            arrived(0, slot, t // 4, t % 4)
        for part, count in ((0, 4), (1, 2)):
            halos.append(remote(
                homes.at[slot, part, pl.ds(0, count), pl.ds(0, 2)],
                homes.at[slot, 4 + part, pl.ds(0, count), pl.ds(0, 2)],
                halo_send.at[slot, part], halo_recv.at[slot, part], me.left,
            ))
            halos[-1].start()
    pass_on(1)

    for slot in range(2):
        for t in range(6, 16):
            arrived(0, slot, t // 4, t % 4)
        for t in range(16):
            arrived(1, slot, t // 4, t % 4)
        for part, count in ((0, 4), (1, 2)):
            landed(homes.at[slot, 4 + part, pl.ds(0, count), pl.ds(0, 2)], halo_recv.at[slot, part])
            landed(field_homes.at[slot, 4 + part, pl.ds(0, count)], field_recv.at[slot, part])
        landed(hits.at[slot, opposite], relay_recv.at[slot])
    landed(hits.at[1, before], ring_recv.at[0, 1])
    landed(hits.at[0, after], ring_recv.at[1, 0])
    for copy in kept:
        copy.wait()
    for copy in ring + relays + halos:
        copy.wait_send()
    for copy in first + second:
        sent(me, *copy)


def traces(mom, seps, fields, products, hits, out, left_t, source, sums):
    f32 = jnp.float32
    tm = lax.axis_index("tm")
    plane, local = tm // 8, tm % 8
    diagonal = local == 0
    m1, m2, m3, m4 = (mom[i] for i in range(4))

    for role in range(2):
        for c in range(2):
            @pl.loop(0, 16)
            def _(part):
                block = hits[role, part // 4, pl.ds(2 * (part % 4), 2), c].reshape(BLK, BLK)
                left_t[role, pl.ds(c * BLK, BLK), pl.ds(pl.multiple_of(part * BLK, BLK), BLK)] = block.T

    @pl.loop(0, 16)
    def _(part):
        block = hits[0, part // 4, pl.ds(2 * (part % 4), 2), 4].reshape(BLK, BLK)
        source[:, pl.ds(pl.multiple_of(part * BLK, BLK), BLK)] = block.T[:16]

    def fold(value):
        return jnp.sum(value, axis=0, keepdims=True)

    @pl.loop(0, SPAN)
    def _(t):
        stamp = (plane * SPAN + t).astype(f32)
        chosen = (source[:1, :].astype(f32) == stamp).astype(f32).astype(jnp.bfloat16)
        totals = [[jnp.zeros((1, BLK), f32) for _ in range(8)] for _ in range(3)]
        for slot in range(2):
            mate = jnp.where(diagonal, slot, 1 - slot)
            right = jnp.concatenate(
                [hits[mate, :, :, 2 + c].reshape(2048, BLK) for c in range(2)], axis=1
            )
            pieces = jnp.dot(left_t[slot] * chosen, right, preferred_element_type=f32)
            w_re = (pieces[:BLK, :BLK] - pieces[BLK:, BLK:]).astype(jnp.bfloat16).astype(f32)
            w_im = (pieces[:BLK, BLK:] + pieces[BLK:, :BLK]).astype(jnp.bfloat16).astype(f32)
            p1 = [fields[slot, t, m1, c].astype(f32).T for c in range(2)]
            p4 = [fields[slot, t, m4, c].astype(f32).T for c in range(2)]
            rt = [products[slot, t, 2 + c].astype(f32) for c in range(2)]
            for k in range(3):
                u = t + seps[k]
                p2 = [fields[mate, u, m2, c].astype(f32) for c in range(2)]
                p3 = [fields[mate, u, m3, c].astype(f32) for c in range(2)]
                s = [products[slot, u, c].astype(f32) for c in range(2)]
                for at, (one, two) in enumerate(
                    ((p1, p2), (p4, p3), (rt, s), ((w_re, w_im), s))
                ):
                    totals[k][2 * at] += fold(one[0] * two[0] - one[1] * two[1])
                    totals[k][2 * at + 1] += fold(one[0] * two[1] + one[1] * two[0])
        for k in range(3):
            sums[3 * t + k] = jnp.concatenate(totals[k], axis=0)

    out[...] = jnp.sum(sums[...], axis=-1)


def reduce(part, out, gather, send, recv):
    me = Place()
    barrier = pltpu.get_barrier_semaphore()
    base = 8 * me.x
    mine = 4 * (me.tm % 8) + me.mode
    others = [(base + n // 4, n % 4) for n in range(32)]
    for n in range(32):
        @pl.when(mine != n)
        def _():
            pl.semaphore_signal(barrier, inc=1, device_id=others[n], device_id_type=MESH)
    pl.semaphore_wait(barrier, 31)
    copies = [(part.at[n // 4], gather.at[mine], send.at[n], recv.at[mine], others[n])
              for n in range(32)]
    for copy in copies:
        send_or_keep(me, *copy)
    for n in range(32):
        landed(gather.at[n], recv.at[n])
    total = jnp.sum(gather[...], axis=0)
    out[...] = total
    out[0:1] = total[0:1] * total[2:3] - total[1:2] * total[3:4]
    out[1:2] = total[0:1] * total[3:4] + total[1:2] * total[2:3]
    for copy in copies:
        sent(me, *copy)


def params(ident=None):
    if ident is None:
        return pltpu.CompilerParams(vmem_limit_bytes=VMEM_LIMIT)
    return pltpu.CompilerParams(
        vmem_limit_bytes=VMEM_LIMIT, collective_id=ident, has_side_effects=True
    )


def on_device(field_codes, scales, mom_index, separations, source_slice, noise_left, noise_right):
    mode = lax.axis_index("mode")
    bf16, f32 = jnp.bfloat16, jnp.float32
    dma = pltpu.SemaphoreType.DMA
    fields = (field_codes.astype(f32) * scales[:, :, None, :, None]).astype(bf16)
    fields = fields.transpose(1, 0, 2, 3, 4)
    mine = lax.dynamic_slice_in_dim(noise_left, mode * 256, 256, axis=2)
    noise = jnp.concatenate(
        [mine, noise_right, jnp.broadcast_to(source_slice.astype(bf16)[:, None, None], (64, 1, 256))],
        axis=1,
    )
    noise = noise.reshape(64, 5, 2, BLK).transpose(2, 1, 0, 3)

    any_spec = pl.BlockSpec(memory_space=ANY)
    smem = pl.BlockSpec(memory_space=pltpu.SMEM)
    vmem = pl.BlockSpec(memory_space=pltpu.VMEM)
    whole, field_homes, hits = pl.pallas_call(
        spread_fields,
        out_shape=(
            jax.ShapeDtypeStruct((2, 2, 1024, 1024), bf16),
            jax.ShapeDtypeStruct((2, 4, 4, 2, 2, BLK, BLK), bf16),
            jax.ShapeDtypeStruct((2, 4, 2, 5, 64, BLK), bf16),
        ),
        in_specs=[any_spec] * 2,
        out_specs=[any_spec] * 3,
        scratch_shapes=[
            pltpu.VMEM((4, 4, 2, 2, 2, BLK, BLK), bf16),
            pltpu.VMEM((4, 4, 5, 64, BLK), bf16),
            dma((2,)), dma((2,)), dma((2,)), dma((2,)),
            dma((2, 2, 4)), dma((4, 4)), dma((4, 4)), dma((2, 4, 2)),
            dma((2, 2, 4)), dma((4, 4)), dma((4, 4)), dma((2, 4, 2)),
        ],
        compiler_params=params(0),
        name="spread_fields",
    )(fields, noise)
    products = pl.pallas_call(
        multiply,
        out_shape=jax.ShapeDtypeStruct((4, 8, 4, BLK, BLK), bf16),
        in_specs=[smem, vmem],
        out_specs=vmem,
        compiler_params=params(),
        name="multiply",
    )(mom_index, whole)
    product_homes, field_homes, hits = pl.pallas_call(
        spread_products,
        out_shape=(
            jax.ShapeDtypeStruct((2, 6, 4, 4, BLK, BLK), bf16),
            jax.ShapeDtypeStruct((2, 6, 4, 2, 2, BLK, BLK), bf16),
            jax.ShapeDtypeStruct((2, 4, 4, 2, 5, 64, BLK), bf16),
        ),
        in_specs=[any_spec] * 3,
        out_specs=[any_spec] * 3,
        scratch_shapes=[
            pltpu.VMEM((2, 2, 4, 4, 2, BLK, BLK), bf16),
            dma((2, 4, 2, 4)), dma((2, 2, 4, 4)), dma((2, 2, 4, 4)), dma((2, 2, 4, 4)),
            dma((2, 2)), dma((2, 2)), dma((2, 2)), dma((2, 2)),
            dma((2, 2)), dma((2, 2)), dma((2,)), dma((2,)), dma((2, 2)),
        ],
        compiler_params=params(1),
        name="spread_products",
    )(products, field_homes, hits)
    part = pl.pallas_call(
        traces,
        out_shape=jax.ShapeDtypeStruct((3 * SPAN, 8), f32),
        in_specs=[smem, smem, vmem, vmem, vmem],
        out_specs=vmem,
        scratch_shapes=[
            pltpu.VMEM((2, 2 * BLK, 2048), bf16),
            pltpu.VMEM((16, 2048), bf16),
            pltpu.VMEM((3 * SPAN, 8, BLK), f32),
        ],
        compiler_params=params(),
        name="traces",
    )(
        mom_index, separations,
        field_homes.reshape(2, 24, 2, 2, BLK, BLK),
        product_homes.reshape(2, 24, 4, BLK, BLK),
        hits.reshape(2, 4, 8, 5, 64, BLK),
    )
    part = jnp.pad(part.reshape(8, 6, 8).transpose(0, 2, 1), ((0, 0), (0, 0), (0, BLK - 6)))
    total = pl.pallas_call(
        reduce,
        out_shape=jax.ShapeDtypeStruct((8, BLK), f32),
        in_specs=[vmem],
        out_specs=vmem,
        scratch_shapes=[pltpu.VMEM((32, 8, BLK), f32), dma((32,)), dma((32,))],
        compiler_params=params(2),
        name="reduce",
    )(part)
    table = total[:, :6].T.reshape(2, 3, 8)
    return table[..., 0:2], table[..., 4:6], table[..., 6:8]


def solution(mesh):
    in_specs = (
        P(None, "tm", None, "mode", None),
        P(None, "tm", "mode"),
        P(),
        P(),
        P("tm"),
        P("tm", None, None),
        P("tm", None, "mode"),
    )
    out_specs = (P("tm", None, None), P("tm", None, None), P("tm", None, None))
    return jax.shard_map(
        on_device, mesh=mesh, in_specs=in_specs, out_specs=out_specs, check_vma=False
    )
```

time: 396 us -> 348 us (0.88)
  blocking collectives: 83.6 us -> 0 us
  Pallas kernels: 302 us -> 337 us
    psum x1 -> x0, blocking collectives: 83.6 us -> none  [on_device(): total = lax.psum(table, ('tm', 'mode'))]
    pallas_call x1 -> x2, Pallas kernels: 92.8 us -> 154 us  [the longest x1 142 us: on_device(): pl.pallas_call(spread_products, out_shape=(jax.ShapeDtypeStruct((2, 6, 4,...]
    pallas_call x1, Pallas kernels: 164 us -> 137 us  [on_device(): pl.pallas_call(spread_fields, out_shape=(jax.ShapeDtypeStruct((2, 2, 1024...]
    convert_element_type x1 -> x0, other arithmetic: 4.94 us -> none  [on_device(): (field_codes.astype(f32) * scales[:, :, None, :, None]).astype(bf16)]
    transpose x0 -> x1, other arithmetic: none -> 4.89 us  [on_device(): fields = fields.transpose(1, 0, 2, 3, 4)]
where the time goes in v2:
time: 348 us
  Pallas kernels  337 us (97%)
  other arithmetic  6.65 us (2%)
    pallas_call x1, Pallas kernels, on_device(): pl.pallas_call(spread_products, out_shape=(jax.ShapeDtypeStruct((2, 6, 4,...  142 us
    pallas_call x1, Pallas kernels, on_device(): pl.pallas_call(spread_fields, out_shape=(jax.ShapeDtypeStruct((2, 2, 1024...  137 us
    pallas_call x1, Pallas kernels, on_device(): pl.pallas_call(traces, out_shape=jax.ShapeDtypeStruct((3 * SPAN, 8), f32)...  30.1 us
    pallas_call x1, Pallas kernels, on_device(): pl.pallas_call(multiply, out_shape=jax.ShapeDtypeStruct((4, 8, 4, BLK, BL...  16.2 us
    pallas_call x1, Pallas kernels, on_device(): pl.pallas_call(reduce, out_shape=jax.ShapeDtypeStruct((8, BLK), f32), in_...  12.2 us

profile of v2, /device:TPU:1, one launch (start us, length us, event | category | flops | bytes accessed | tf_op | source)
XLA Modules:
  0.0 347.9 jit_solution(8433567559772197609)
XLA Ops:
  0.6 0.0 copy-start
  0.6 0.7 convert_element_type.13
  1.4 0.7 copy.17
  2.0 0.1 broadcast_in_dim.2
  2.2 0.0 copy-done
  2.2 0.1 constant_dynamic-slice_fusion
  2.3 1.1 pad_maximum_fusion
  3.3 0.1 reshape.34
  3.5 4.9 %fusion.fields = bf16[2,2,2,256,1024]{4,3,2,1,0:T(8,128)(2,1)} fusion(bf16[2,2,2,256,1024]{4,3,2,1,0:T(8,128)(2,1)} %param.7, f32[2,2,256]{2,0,1:T(2,128)S(1)} %copy.17), kind=kLoop, calls=%fused_computation.1 | loop fusion | flops 6291456 | bytes 8392704 | tf_op jit(solution)/shard_map/transpose | solution.py:427
  8.3 0.0 copy-start.1
  8.3 136.6 %spread_fields.1 = (bf16[2,2,1024,1024]{3,2,1,0:T(8,128)(2,1)}, bf16[2,4,4,2,2,128,128]{6,5,4,3,2,1,0:T(8,128)(2,1)}, bf16[2,4,2,5,64,128]{5,4,3,2,1,0:T(8,128)(2,1)S(1)}) custom-call(bf16[2,2,2,256,1024]{4,3,2,1,0:T(8,128)(2,1)} %fusion.fields, bf16[2,5,64,128]{3,2,1,0:T(8,128)(2,1)S(1)} %bitcast.11), custom_call_target="tpu_custom_call" | custom-call | tf_op jit(solution)/shard_map/spread_fields/pallas_call | solution.py:438
  145.0 0.0 copy-done.1
  145.0 16.2 %multiply.1.products = bf16[4,8,4,128,128]{4,3,2,1,0:T(8,128)(2,1)} custom-call(s32[4]{0:T(128)S(1)} %copy-done.1, bf16[2,2,1024,1024]{3,2,1,0:T(8,128)(2,1)} %get-tuple-element.9.whole), custom_call_target="tpu_custom_call" | custom-call | tf_op jit(solution)/shard_map/multiply/pallas_call | solution.py:457
  161.1 0.0 copy-start.2
  161.1 142.1 %spread_products.1 = (bf16[2,6,4,4,128,128]{5,4,3,2,1,0:T(8,128)(2,1)}, bf16[2,6,4,2,2,128,128]{6,5,4,3,2,1,0:T(8,128)(2,1)}, bf16[2,4,4,2,5,64,128]{6,5,4,3,2,1,0:T(8,128)(2,1)}) custom-call(bf16[4,8,4,128,128]{4,3,2,1,0:T(8,128)(2,1)} %multiply.1.products, bf16[2,4,4,2,2,128,128]{6,5,4,3,2,1,0:T(8,128)(2,1)} %get-tuple-element.10.fields, ...), custom_call_target="tpu_custom_call" | custom-call | tf_op jit(solution)/shard_map/spread_products/pallas_call | solution.py:465
  303.3 0.0 copy-done.2
  303.3 30.1 %traces.1 = f32[48,8]{1,0:T(8,128)S(1)} custom-call(s32[4]{0:T(128)S(1)} %copy-done.1, s32[3]{0:T(128)S(1)} %copy-done.2, bf16[2,24,2,2,128,128]{5,4,3,2,1,0:T(8,128)(2,1)} %bitcast.13, bf16[2,24,4,128,128]{4,3,2,1,0:T(8,128)(2,1)} %bitcast.12, bf16[2,4,8,5,64,128]{5,4,3,2,1,0:T(8,128)(2,1)} %bitcast.14), custom_call_target="tpu_custom_call" | custom-call | tf_op jit(solution)/shard_map/traces/pallas_call | solution.py:483
  333.4 0.1 copy.21
  333.5 12.2 %reduce.1 = f32[8,128]{1,0:T(8,128)S(1)} custom-call(f32[8,8,128]{2,1,0:T(8,128)S(1)} %pad.4.part), custom_call_target="tpu_custom_call" | custom-call | tf_op jit(solution)/shard_map/reduce/pallas_call | solution.py:502
  345.7 0.1 copy.22
  345.8 0.1 fusion.1
  345.9 0.7 copy.25
  346.6 0.7 copy.24
  347.2 0.7 copy.23
  (5 shorter events, 0.1 us)
Async XLA Ops:
  0.6 1.5 copy-start
  8.3 136.6 %copy-start.1 = (s32[4]{0:T(128)S(1)}, s32[4]{0:T(128)}, u32[]{:S(2)}) copy-start(s32[4]{0:T(128)} %mom.3) | copy-start | bytes 52
  161.1 142.1 %copy-start.2 = (s32[3]{0:T(128)S(1)}, s32[3]{0:T(128)}, u32[]{:S(2)}) copy-start(s32[3]{0:T(128)} %seps.1) | copy-start | bytes 40

commit v3 on v2

v3 whole, which is shorter than its diff:
```python
import jax
import jax.numpy as jnp
from jax import lax
from jax.experimental import pallas as pl
from jax.experimental.pallas import tpu as pltpu
from jax.sharding import PartitionSpec as P

MESH = pl.DeviceIdType.MESH
ANY = pl.ANY
BLK = 128
SPAN = 16
VMEM_LIMIT = 56 * 1024 * 1024


def home(i, half, e, same):
    if same:
        if e == 0:
            unit, slot = i % 2, i // 2
        elif e == 1:
            unit, slot = 4 + i, 0
        elif e == 2:
            unit, slot = 2 + i % 2, i // 2
        else:
            unit, slot = 4 + (i + 3) % 4, 1
        return unit // 2, 0, half, unit % 2, slot, 4 * half + (i + e) % 4
    upper, lower = i + half * (e - i), e + half * (i - e)
    return upper, 1, (i + e) % 2, lower // 2, half, 4 * (1 - half) + e


def blocks_of(z, lo, hi, core):
    if z < 2:
        near = (core, core + 2)
    elif z == 2:
        near = (core, core + 1)
    else:
        near = (2 + core, (3 + core) % 4)
    far = (z, 4 + 2 * core + (hi + z) % 2)
    return tuple(4 * hi * (1 - lo) + n + lo * (f - n) for n, f in zip(near, far))


class Place:
    def __init__(self):
        self.tm = lax.axis_index("tm")
        self.mode = lax.axis_index("mode")
        self.x, self.z, self.lo = self.tm // 8, (self.tm // 2) % 4, self.tm % 2
        self.hi, self.core = self.mode // 2, self.mode % 2
        self.right = ((self.tm + 8) % 32, self.mode)
        self.left = ((self.tm + 24) % 32, self.mode)

    def at(self, z, lo, hi, core):
        return (8 * self.x + 2 * z + lo, 2 * hi + core)

    def is_here(self, device):
        return jnp.logical_and(device[0] == self.tm, device[1] == self.mode)


def greet(place):
    barrier = pltpu.get_barrier_semaphore()

    def signal(device):
        pl.semaphore_signal(barrier, inc=1, device_id=device, device_id_type=MESH)

    for core in range(2):
        for z in range(4):

            @pl.when(jnp.logical_or(place.z != z, place.core != core))
            def _():
                signal(place.at(z, place.lo, place.hi, core))

        for y in range(4):

            @pl.when(jnp.logical_or(place.lo != y // 2, place.hi != y % 2))
            def _():
                signal(place.at(place.z, y // 2, y % 2, core))

    signal(place.right)
    signal(place.left)
    pl.semaphore_wait(barrier, 15)


def remote(src, dst, send, recv, device):
    return pltpu.make_async_remote_copy(
        src_ref=src, dst_ref=dst, send_sem=send, recv_sem=recv,
        device_id=device, device_id_type=MESH,
    )


def send_or_keep(place, src, dst, send, recv, device):
    here = place.is_here(device)

    @pl.when(jnp.logical_not(here))
    def _():
        remote(src, dst, send, recv, device).start()

    @pl.when(here)
    def _():
        pltpu.make_async_copy(src, dst, recv).start()


def sent(place, src, dst, send, recv, device):
    @pl.when(jnp.logical_not(place.is_here(device)))
    def _():
        remote(src, dst, send, recv, device).wait_send()


def landed(ref, sem):
    pltpu.make_async_copy(ref, ref, sem).wait()


def pair_sums(one, two):
    real = one[0] * two[0] - one[1] * two[1]
    imag = one[0] * two[1] + one[1] * two[0]
    return [jnp.sum(value, axis=0, keepdims=True) for value in (real, imag)]


def contract(
    mom, seps, fields, noise, out,
    whole, homes, mid_y, mid_z, products, mid, product_homes, mid_hits, hits,
    left_t, source, weights, box_sums, product_sums,
    asm_send, asm_recv, fwd_send, fwd_recv,
    hit_z_send, hit_z_recv, hit_y_send, hit_y_recv,
    ring_send, ring_recv, relay_send, relay_recv,
    near_send, cross_z_send, cross_z_recv, cross_y_send,
    whole_z_send, whole_y_send, whole_y_recv, whole_pass_send, home_recv,
    send1, recv1, send2, recv2,
    field_send, field_recv, halo_send, halo_recv,
):
    f32, bf16 = jnp.float32, jnp.bfloat16
    me = Place()
    greet(me)
    flip = me.tm + 1 - 2 * me.lo
    when = 2 * (1 - me.lo) + me.hi
    sends = []

    def start(*copy, only=None):
        sends.append((copy, only))
        if only is None:
            send_or_keep(me, *copy)
        else:

            @pl.when(me.lo == only)
            def _():
                send_or_keep(me, *copy)

    def tile(n):
        return pl.ds(n * BLK if isinstance(n, int) else pl.multiple_of(n * BLK, BLK), BLK)

    def rows_of(block):
        return whole.at[:, :, pl.ds(pl.multiple_of(block * 256, 256), 256), :]

    assembly = [
        remote(fields.at[s], rows_of(me.mode), asm_send.at[s], asm_recv.at[me.hi],
               (flip, 2 * s + me.core))
        for s in range(2)
    ]
    for copy in assembly:
        copy.start()

    for a in range(2):
        for same in (False, True):
            for e in range(4):
                z, lo, hi, core, slot, col = home(2 * me.core + a, me.hi, e, same)
                group = slot if same else 2 + hi
                start(noise.at[a], mid_hits.at[group, me.z], hit_z_send.at[a, int(same), e],
                      hit_z_recv.at[group, me.z], me.at(z, me.lo, me.hi, core))

    def half_way(s, a, z, core, col, e, group):
        start(fields.at[s, :, :, tile(a), tile(col)], mid_y.at[group, me.z],
              cross_z_send.at[a, e], cross_z_recv.at[group, me.z], me.at(z, me.lo, me.hi, core))

    for a in range(2):
        row = 2 * me.core + a
        for e in range(4):
            z, _, hi, core, slot, col = home(row, me.hi, e, True)
            far = home(row, me.hi, e, False)

            def pick(one, two):
                return one + me.lo * (two - one)

            half_way(pick(1 - far[2], 1 - me.hi), a, pick(far[0], z), pick(far[3], core),
                     pick(far[5], col), e, pick(far[2], slot))
        for e in range(4):
            z, _, hi, core, slot, col = home(row, me.hi, e, True)
            for s in range(2):

                start(fields.at[s, :, :, tile(a), tile(col)], homes.at[slot, me.z, s],
                      near_send.at[s, a, e], home_recv.at[slot, me.z, s],
                      me.at(z, 0, me.hi, core), only=0)

        for b in range(2):
            other = 2 * b + (me.hi + a) % 2
            z, _, hi, core, slot, col = home(row, me.hi, other, False)
            for s in range(2):

                start(fields.at[s, :, :, tile(a), tile(col)], homes.at[slot, me.z, 2 + s],
                      near_send.at[s, a, 4 + b], home_recv.at[slot, me.z, 2 + s],
                      me.at(z, 1, me.hi, core), only=1)

    for z in range(4):
        for group in range(4):
            if group < 2:
                slot, device = group, me.at(me.z, 0, me.hi, me.core)
            else:
                slot, device = me.hi, me.at(me.z, 1, group - 2, me.core)
            landed(mid_hits.at[group, z], hit_z_recv.at[group, z])
            start(mid_hits.at[group, z], hits.at[slot, me.x, z, me.lo],
                  hit_y_send.at[group, z], hit_y_recv.at[slot, z, me.lo], device)

    for slot in range(2):
        for z in range(4):
            for lo in range(2):
                landed(hits.at[slot, me.x, z, lo], hit_y_recv.at[slot, z, lo])
    ring = []
    for slot in range(2):
        own = hits.at[slot, me.x]
        ring.append(remote(own, own, ring_send.at[0, slot], ring_recv.at[0, slot], me.right))
        ring.append(remote(own, own, ring_send.at[1, slot], ring_recv.at[1, slot], me.left))
    for copy in ring:
        copy.start()

    forwards = []
    for h in range(2):
        block = rows_of(2 * h + me.core)
        landed(block, asm_recv.at[h])
        forwards.append(remote(block, block, fwd_send.at[h], fwd_recv.at[h],
                               (me.tm, me.mode + 1 - 2 * me.core)))
        forwards[-1].start()

    for z in range(4):
        for group in range(2):
            landed(mid_y.at[group, z], cross_z_recv.at[group, z])
            lo, hi = 1 - me.lo, group + me.lo * (me.hi - group)
            slot = me.hi + me.lo * (group - me.hi)
            t = 2 * me.lo + (1 - group) + me.lo * (group - me.hi)
            start(mid_y.at[group, z], homes.at[slot, z, t], cross_y_send.at[group, z],
                  home_recv.at[slot, z, t], me.at(me.z, lo, hi, me.core))

    before, after, opposite = (me.x + 3) % 4, (me.x + 1) % 4, (me.x + 2) % 4
    relays = []
    for slot in range(2):
        landed(hits.at[slot, before], ring_recv.at[0, slot])
        relays.append(remote(hits.at[slot, before], hits.at[slot, before], relay_send.at[slot],
                             relay_recv.at[slot], me.right))
        relays[-1].start()

    for h in range(2):
        landed(rows_of(2 * h + 1 - me.core), fwd_recv.at[h])
    for hi in range(2):
        for z in range(4):
            pair = blocks_of(z, 1, hi, me.core)
            row, col = pair[1 - hi], pair[hi]

            start(whole.at[:, :, tile(row), tile(col)], mid_z.at[me.hi, z],
                  whole_y_send.at[hi, z], whole_y_recv.at[me.hi, z],
                  me.at(me.z, 1, hi, me.core), only=0)
    for z in range(4):
        pair = blocks_of(z, me.lo, me.hi, me.core)
        for slot in range(2):
            row, col = pair[slot], pair[1 - slot]
            if z == 0:
                col = col + (1 - me.lo) * (row - col)
            start(whole.at[:, :, tile(row), tile(col)], homes.at[slot, me.z, when],
                  whole_z_send.at[z, slot], home_recv.at[slot, me.z, when],
                  me.at(z, me.lo, me.hi, me.core))

    base = pl.multiple_of(me.core * 512, 512)
    m1, m2, m3, m4 = (mom[i] for i in range(4))

    def cdot(ar, ai, br, bi):
        def dot(a, b):
            return jnp.dot(a, b, preferred_element_type=f32)

        return dot(ar, br) - dot(ai, bi), dot(ar, bi) + dot(ai, br)

    @pl.loop(0, 4)
    def _(pair):
        cols = pl.ds(pl.multiple_of(pair * 256, 256), 256)
        rows = pl.ds(base, 512)
        parts = cdot(whole[m2, 0, rows, :], whole[m2, 1, rows, :],
                     whole[m3, 0, :, cols], whole[m3, 1, :, cols])
        for c in range(2):
            for a in range(4):
                for b in range(2):
                    piece = parts[c][a * BLK:(a + 1) * BLK, b * BLK:(b + 1) * BLK]
                    products[0, a, 2 * pair + b, c] = piece.astype(bf16)

    def right_product():
        @pl.loop(0, 4)
        def _(step):
            pair, half = step // 2, step % 2
            cols = pl.ds(pl.multiple_of(base + pair * 256, 256), 256)
            rows = pl.ds(pl.multiple_of(half * 512, 512), 512)
            parts = cdot(whole[m4, 0, rows, :], whole[m4, 1, rows, :],
                         whole[m1, 0, :, cols], whole[m1, 1, :, cols])
            for c in range(2):
                for a in range(2):
                    for b in range(4):
                        piece = parts[c][b * BLK:(b + 1) * BLK, a * BLK:(a + 1) * BLK]
                        products[1, 2 * pair + a, 4 * half + b, c] = piece.T.astype(bf16)

    def send_products(p):
        for i in range(4):
            for same in (False, True):
                for e in range(4):
                    z, lo, hi, core, slot, col = home(i, me.core, e, same)

                    def either(one, two):
                        return one + slot * (two - one)

                    device = me.at(either(me.z, z), either(lo, me.lo), either(hi, me.hi), core)
                    at = (p, slot, either(z, 2 * lo + hi), either(when, me.z))
                    start(products.at[p, i, col], mid.at[at], send1.at[p, i, int(same), e],
                          recv1.at[at], device)

    def pass_on(p):
        for j in range(4):
            for k in range(4):
                landed(mid.at[p, 0, k, j], recv1.at[p, 0, k, j])
                start(mid.at[p, 0, k, j], product_homes.at[p, 0, me.z, j],
                      send2.at[p, 0, k, j], recv2.at[p, 0, me.z, j],
                      me.at(k, me.lo, me.hi, me.core))
                landed(mid.at[p, 1, k, j], recv1.at[p, 1, k, j])
                start(mid.at[p, 1, k, j], product_homes.at[p, 1, j, when],
                      send2.at[p, 1, k, j], recv2.at[p, 1, j, when],
                      me.at(me.z, k // 2, k % 2, me.core))

    send_products(0)

    for hi in range(2):
        for z in range(4):

            @pl.when(me.lo == 1)
            def _():
                landed(mid_z.at[hi, z], whole_y_recv.at[hi, z])

            start(mid_z.at[hi, z], homes.at[1 - me.hi, me.z, 2 + hi],
                  whole_pass_send.at[hi, z], home_recv.at[1 - me.hi, me.z, 2 + hi],
                  me.at(z, 1, me.hi, me.core), only=1)

    right_product()
    send_products(1)

    halos = []
    parts = ((0, 4), (1, 2))
    for slot in range(2):
        for t in range(6):
            landed(homes.at[slot, t // 4, t % 4], home_recv.at[slot, t // 4, t % 4])
        for part, count in parts:
            halos.append(remote(
                homes.at[slot, part, pl.ds(0, count)], homes.at[slot, 4 + part, pl.ds(0, count)],
                field_send.at[slot, part], field_recv.at[slot, part], me.left,
            ))
            halos[-1].start()

    pass_on(0)

    for slot in range(2):
        landed(hits.at[slot, after], ring_recv.at[1, slot])
        landed(hits.at[slot, opposite], relay_recv.at[slot])
    for role in range(2):
        for c in range(2):

            @pl.loop(0, 16)
            def _(part):
                block = hits[role, part // 4, part % 4, :, c].reshape(BLK, BLK)
                left_t[role, pl.ds(c * BLK, BLK), tile(part)] = block.T

    @pl.loop(0, 16)
    def _(part):
        block = hits[0, part // 4, part % 4, :, 4].reshape(BLK, BLK)
        source[:, tile(part)] = block.T[:16]

    diagonal = jnp.logical_and(me.lo == 0, me.z == 0)

    @pl.loop(0, SPAN)
    def _(t):
        stamp = (me.x * SPAN + t).astype(f32)
        chosen = (source[:1, :].astype(f32) == stamp).astype(f32).astype(bf16)
        for slot in range(2):
            mate = jnp.where(diagonal, slot, 1 - slot)
            right = jnp.concatenate(
                [hits[mate, :, :, :, 2 + c].reshape(2048, BLK) for c in range(2)], axis=1
            )
            pieces = jnp.dot(left_t[slot] * chosen, right, preferred_element_type=f32)
            weights[slot, t, 0] = (pieces[:BLK, :BLK] - pieces[BLK:, BLK:]).astype(bf16)
            weights[slot, t, 1] = (pieces[:BLK, BLK:] + pieces[BLK:, :BLK]).astype(bf16)

    for slot in range(2):
        for t in range(6):
            landed(product_homes.at[0, slot, t // 4, t % 4], recv2.at[0, slot, t // 4, t % 4])
        for part, count in parts:
            halos.append(remote(
                product_homes.at[0, slot, part, pl.ds(0, count)],
                product_homes.at[0, slot, 4 + part, pl.ds(0, count)],
                halo_send.at[slot, part], halo_recv.at[slot, part], me.left,
            ))
            halos[-1].start()
    pass_on(1)

    for slot in range(2):
        for t in range(6, 16):
            landed(homes.at[slot, t // 4, t % 4], home_recv.at[slot, t // 4, t % 4])
        for part, count in parts:
            landed(homes.at[slot, 4 + part, pl.ds(0, count)], field_recv.at[slot, part])

    @pl.loop(0, SPAN)
    def _(t):
        totals = [[jnp.zeros((1, BLK), f32) for _ in range(4)] for _ in range(3)]
        for slot in range(2):
            mate = jnp.where(diagonal, slot, 1 - slot)
            p1 = [homes[slot, t // 4, t % 4, m1, c].astype(f32).T for c in range(2)]
            p4 = [homes[slot, t // 4, t % 4, m4, c].astype(f32).T for c in range(2)]
            for k in range(3):
                u = t + seps[k]
                p2 = [homes[mate, u // 4, u % 4, m2, c].astype(f32) for c in range(2)]
                p3 = [homes[mate, u // 4, u % 4, m3, c].astype(f32) for c in range(2)]
                new = pair_sums(p1, p2) + pair_sums(p4, p3)
                totals[k] = [a + b for a, b in zip(totals[k], new)]
        for k in range(3):
            box_sums[3 * t + k] = jnp.concatenate(totals[k], axis=0)

    for slot in range(2):
        for t in range(6, 16):
            landed(product_homes.at[0, slot, t // 4, t % 4], recv2.at[0, slot, t // 4, t % 4])
        for t in range(16):
            landed(product_homes.at[1, slot, t // 4, t % 4], recv2.at[1, slot, t // 4, t % 4])
        for part, count in parts:
            landed(product_homes.at[0, slot, 4 + part, pl.ds(0, count)], halo_recv.at[slot, part])

    @pl.loop(0, SPAN)
    def _(t):
        totals = [[jnp.zeros((1, BLK), f32) for _ in range(4)] for _ in range(3)]
        for slot in range(2):
            rt = [product_homes[1, slot, t // 4, t % 4, c].astype(f32) for c in range(2)]
            w = [weights[slot, t, c].astype(f32) for c in range(2)]
            for k in range(3):
                u = t + seps[k]
                s = [product_homes[0, slot, u // 4, u % 4, c].astype(f32) for c in range(2)]
                new = pair_sums(rt, s) + pair_sums(w, s)
                totals[k] = [a + b for a, b in zip(totals[k], new)]
        for k in range(3):
            product_sums[3 * t + k] = jnp.concatenate(totals[k], axis=0)

    out[:, 0:4] = jnp.sum(box_sums[...], axis=-1)
    out[:, 4:8] = jnp.sum(product_sums[...], axis=-1)

    for copy in assembly + forwards + ring + relays + halos:
        copy.wait_send()
    for copy, only in sends:
        if only is None:
            sent(me, *copy)
        else:

            @pl.when(me.lo == only)
            def _():
                sent(me, *copy)


def reduce(part, out, gather, send, recv):
    me = Place()
    barrier = pltpu.get_barrier_semaphore()
    base = 8 * me.x
    mine = 4 * (me.tm % 8) + me.mode
    others = [(base + n // 4, n % 4) for n in range(32)]
    for n in range(32):
        @pl.when(mine != n)
        def _():
            pl.semaphore_signal(barrier, inc=1, device_id=others[n], device_id_type=MESH)
    pl.semaphore_wait(barrier, 31)
    copies = [(part.at[n // 4], gather.at[mine], send.at[n], recv.at[mine], others[n])
              for n in range(32)]
    for copy in copies:
        send_or_keep(me, *copy)
    for n in range(32):
        landed(gather.at[n], recv.at[n])
    total = jnp.sum(gather[...], axis=0)
    out[...] = total
    out[0:1] = total[0:1] * total[2:3] - total[1:2] * total[3:4]
    out[1:2] = total[0:1] * total[3:4] + total[1:2] * total[2:3]
    for copy in copies:
        sent(me, *copy)


def params(ident):
    return pltpu.CompilerParams(
        vmem_limit_bytes=VMEM_LIMIT, collective_id=ident, has_side_effects=True
    )


def on_device(field_codes, scales, mom_index, separations, source_slice, noise_left, noise_right):
    mode = lax.axis_index("mode")
    bf16, f32 = jnp.bfloat16, jnp.float32
    dma = pltpu.SemaphoreType.DMA
    fields = (field_codes.astype(f32) * scales[:, :, None, :, None]).astype(bf16)
    fields = fields.transpose(1, 0, 2, 3, 4)
    mine = lax.dynamic_slice_in_dim(noise_left, mode * 256, 256, axis=2)
    noise = jnp.concatenate(
        [mine, noise_right, jnp.broadcast_to(source_slice.astype(bf16)[:, None, None], (64, 1, 256))],
        axis=1,
    )
    noise = noise.reshape(64, 5, 2, BLK).transpose(2, 1, 0, 3)

    any_spec = pl.BlockSpec(memory_space=ANY)
    smem = pl.BlockSpec(memory_space=pltpu.SMEM)
    vmem = pl.BlockSpec(memory_space=pltpu.VMEM)
    dims = lambda *shape: pltpu.VMEM(shape, bf16)
    part = pl.pallas_call(
        contract,
        out_shape=jax.ShapeDtypeStruct((3 * SPAN, 8), f32),
        in_specs=[smem, smem, any_spec, any_spec],
        out_specs=vmem,
        scratch_shapes=[
            dims(2, 2, 1024, 1024),
            dims(2, 6, 4, 2, 2, BLK, BLK),
            dims(2, 4, 2, 2, BLK, BLK),
            dims(2, 4, 2, 2, BLK, BLK),
            dims(2, 4, 8, 2, BLK, BLK),
            dims(2, 2, 4, 4, 2, BLK, BLK),
            dims(2, 2, 6, 4, 2, BLK, BLK),
            dims(4, 4, 5, 64, BLK),
            dims(2, 4, 4, 2, 5, 64, BLK),
            dims(2, 2 * BLK, 2048),
            dims(16, 2048),
            dims(2, SPAN, 2, BLK, BLK),
            pltpu.VMEM((3 * SPAN, 4, BLK), f32),
            pltpu.VMEM((3 * SPAN, 4, BLK), f32),
            dma((2,)), dma((2,)), dma((2,)), dma((2,)),
            dma((2, 2, 4)), dma((4, 4)), dma((4, 4)), dma((2, 4, 2)),
            dma((2, 2)), dma((2, 2)), dma((2,)), dma((2,)),
            dma((2, 2, 6)), dma((2, 4)), dma((2, 4)), dma((2, 4)),
            dma((4, 2)), dma((2, 4)), dma((2, 4)), dma((2, 4)), dma((2, 4, 4)),
            dma((2, 4, 2, 4)), dma((2, 2, 4, 4)), dma((2, 2, 4, 4)), dma((2, 2, 4, 4)),
            dma((2, 2)), dma((2, 2)), dma((2, 2)), dma((2, 2)),
        ],
        compiler_params=params(0),
        name="contract",
    )(mom_index, separations, fields, noise)
    part = jnp.pad(part.reshape(8, 6, 8).transpose(0, 2, 1), ((0, 0), (0, 0), (0, BLK - 6)))
    total = pl.pallas_call(
        reduce,
        out_shape=jax.ShapeDtypeStruct((8, BLK), f32),
        in_specs=[vmem],
        out_specs=vmem,
        scratch_shapes=[pltpu.VMEM((32, 8, BLK), f32), dma((32,)), dma((32,))],
        compiler_params=params(2),
        name="reduce",
    )(part)
    table = total[:, :6].T.reshape(2, 3, 8)
    return table[..., 0:2], table[..., 4:6], table[..., 6:8]


def solution(mesh):
    in_specs = (
        P(None, "tm", None, "mode", None),
        P(None, "tm", "mode"),
        P(),
        P(),
        P("tm"),
        P("tm", None, None),
        P("tm", None, "mode"),
    )
    out_specs = (P("tm", None, None), P("tm", None, None), P("tm", None, None))
    return jax.shard_map(
        on_device, mesh=mesh, in_specs=in_specs, out_specs=out_specs, check_vma=False
    )
```

time: 348 us -> 223 us (0.64)
  Pallas kernels: 337 us -> 209 us
    pallas_call x4 -> x1, Pallas kernels: 325 us -> 181 us  [on_device(): pl.pallas_call(contract, out_shape=jax.ShapeDtypeStruct((3 * SPAN, 8), f3...]
    pallas_call x1, Pallas kernels: 12.2 us -> 27.8 us  [on_device(): pl.pallas_call(reduce, out_shape=jax.ShapeDtypeStruct((8, BLK), f32), in_...]
where the time goes in v3:
time: 223 us; the launch traced here: 222 us
  Pallas kernels  209 us (94%)
  other arithmetic  6.62 us (3%)
  local copies, waits for them, and re-layouts  6.01 us (3%)
    pallas_call x1, Pallas kernels, on_device(): pl.pallas_call(contract, out_shape=jax.ShapeDtypeStruct((3 * SPAN, 8), f3...  181 us
    pallas_call x1, Pallas kernels, on_device(): pl.pallas_call(reduce, out_shape=jax.ShapeDtypeStruct((8, BLK), f32), in_...  27.8 us
    transpose x1, other arithmetic, on_device(): fields = fields.transpose(1, 0, 2, 3, 4)  4.86 us

profile of v3, /device:TPU:1, one launch (start us, length us, event | category | flops | bytes accessed | tf_op | source)
XLA Modules:
  0.0 222.3 jit_solution(1876402172384547272)
XLA Ops:
  0.6 0.0 copy-start
  0.6 0.7 convert_element_type.13
  1.4 0.7 copy.17
  2.0 0.1 broadcast_in_dim.2
  2.2 0.0 copy-done
  2.2 0.1 constant_dynamic-slice_fusion
  2.3 1.1 pad_maximum_fusion
  3.3 0.1 reshape.22
  3.4 0.7 copy.32
  4.1 4.9 %fusion.fields = bf16[2,2,2,256,1024]{4,3,2,1,0:T(8,128)(2,1)} fusion(bf16[2,2,2,256,1024]{4,3,2,1,0:T(8,128)(2,1)} %param.7, f32[2,2,256]{2,0,1:T(2,128)S(1)} %copy.17), kind=kLoop, calls=%fused_computation.1 | loop fusion | flops 6291456 | bytes 8392704 | tf_op jit(solution)/shard_map/transpose | solution.py:495
  9.0 181.2 %contract.1 = f32[48,8]{1,0:T(8,128)} custom-call(s32[4]{0:T(128)} %mom.1, s32[3]{0:T(128)} %seps.1, bf16[2,2,2,256,1024]{4,3,2,1,0:T(8,128)(2,1)} %fusion.fields, bf16[2,5,64,128]{3,2,1,0:T(8,128)(2,1)} %bitcast.8), custom_call_target="tpu_custom_call" | custom-call | tf_op jit(solution)/shard_map/contract/pallas_call | solution.py:507
  190.2 0.7 reshape.23
  191.0 0.1 copy.21
  191.1 0.6 pad.4.part
  191.7 27.8 %reduce.1 = f32[8,128]{1,0:T(8,128)} custom-call(f32[8,8,128]{2,1,0:T(8,128)} %pad.4.part), custom_call_target="tpu_custom_call" | custom-call | tf_op jit(solution)/shard_map/reduce/pallas_call | solution.py:539
  219.5 0.7 slice_bitcast_fusion
  220.1 0.1 copy.22
  220.2 0.1 fusion.1
  220.3 0.7 copy.25
  221.0 0.7 copy.24
  221.7 0.7 copy.23
  (1 shorter events, 0.0 us)
Async XLA Ops:
  0.6 1.5 copy-start

commit v4 on v3

--- a/solution.py
+++ b/solution.py
@@ -60,22 +60,16 @@
     def signal(device):
         pl.semaphore_signal(barrier, inc=1, device_id=device, device_id_type=MESH)
 
-    for core in range(2):
-        for z in range(4):
-
-            @pl.when(jnp.logical_or(place.z != z, place.core != core))
-            def _():
-                signal(place.at(z, place.lo, place.hi, core))
-
-        for y in range(4):
-
-            @pl.when(jnp.logical_or(place.lo != y // 2, place.hi != y % 2))
-            def _():
-                signal(place.at(place.z, y // 2, y % 2, core))
+    for n in range(32):
+        device = (8 * place.x + n // 4, n % 4)
+
+        @pl.when(jnp.logical_not(place.is_here(device)))
+        def _():
+            signal(device)
 
     signal(place.right)
     signal(place.left)
-    pl.semaphore_wait(barrier, 15)
+    pl.semaphore_wait(barrier, 33)
 
 
 def remote(src, dst, send, recv, device):
@@ -115,20 +109,21 @@
 
 def contract(
     mom, seps, fields, noise, out,
-    whole, homes, mid_y, mid_z, products, mid, product_homes, mid_hits, hits,
-    left_t, source, weights, box_sums, product_sums,
+    whole, homes, mid_y, mid_z, products, mid, s_homes, r_homes, mid_hits, hits,
+    left_t, source, weights, box_sums, cross_sums, noise_sums, tiles, gather,
     asm_send, asm_recv, fwd_send, fwd_recv,
     hit_z_send, hit_z_recv, hit_y_send, hit_y_recv,
     ring_send, ring_recv, relay_send, relay_recv,
     near_send, cross_z_send, cross_z_recv, cross_y_send,
     whole_z_send, whole_y_send, whole_y_recv, whole_pass_send, home_recv,
     send1, recv1, send2, recv2,
-    field_send, field_recv, halo_send, halo_recv,
+    field_send, field_recv, halo_send, halo_recv, sum_send, sum_recv,
 ):
     f32, bf16 = jnp.float32, jnp.bfloat16
     me = Place()
     greet(me)
     flip = me.tm + 1 - 2 * me.lo
+    tiles[...] = jnp.zeros_like(tiles)
     when = 2 * (1 - me.lo) + me.hi
     sends = []
 
@@ -206,18 +201,6 @@
             start(mid_hits.at[group, z], hits.at[slot, me.x, z, me.lo],
                   hit_y_send.at[group, z], hit_y_recv.at[slot, z, me.lo], device)
 
-    for slot in range(2):
-        for z in range(4):
-            for lo in range(2):
-                landed(hits.at[slot, me.x, z, lo], hit_y_recv.at[slot, z, lo])
-    ring = []
-    for slot in range(2):
-        own = hits.at[slot, me.x]
-        ring.append(remote(own, own, ring_send.at[0, slot], ring_recv.at[0, slot], me.right))
-        ring.append(remote(own, own, ring_send.at[1, slot], ring_recv.at[1, slot], me.left))
-    for copy in ring:
-        copy.start()
-
     forwards = []
     for h in range(2):
         block = rows_of(2 * h + me.core)
@@ -225,6 +208,18 @@
         forwards.append(remote(block, block, fwd_send.at[h], fwd_recv.at[h],
                                (me.tm, me.mode + 1 - 2 * me.core)))
         forwards[-1].start()
+
+    for slot in range(2):
+        for z in range(4):
+            for lo in range(2):
+                landed(hits.at[slot, me.x, z, lo], hit_y_recv.at[slot, z, lo])
+    ring = []
+    for slot in range(2):
+        own = hits.at[slot, me.x]
+        ring.append(remote(own, own, ring_send.at[0, slot], ring_recv.at[0, slot], me.right))
+        ring.append(remote(own, own, ring_send.at[1, slot], ring_recv.at[1, slot], me.left))
+    for copy in ring:
+        copy.start()
 
     for z in range(4):
         for group in range(2):
@@ -234,14 +229,6 @@
             t = 2 * me.lo + (1 - group) + me.lo * (group - me.hi)
             start(mid_y.at[group, z], homes.at[slot, z, t], cross_y_send.at[group, z],
                   home_recv.at[slot, z, t], me.at(me.z, lo, hi, me.core))
-
-    before, after, opposite = (me.x + 3) % 4, (me.x + 1) % 4, (me.x + 2) % 4
-    relays = []
-    for slot in range(2):
-        landed(hits.at[slot, before], ring_recv.at[0, slot])
-        relays.append(remote(hits.at[slot, before], hits.at[slot, before], relay_send.at[slot],
-                             relay_recv.at[slot], me.right))
-        relays[-1].start()
 
     for h in range(2):
         landed(rows_of(2 * h + 1 - me.core), fwd_recv.at[h])
@@ -316,11 +303,11 @@
         for j in range(4):
             for k in range(4):
                 landed(mid.at[p, 0, k, j], recv1.at[p, 0, k, j])
-                start(mid.at[p, 0, k, j], product_homes.at[p, 0, me.z, j],
+                start(mid.at[p, 0, k, j], (s_homes, r_homes)[p].at[0, me.z, j],
                       send2.at[p, 0, k, j], recv2.at[p, 0, me.z, j],
                       me.at(k, me.lo, me.hi, me.core))
                 landed(mid.at[p, 1, k, j], recv1.at[p, 1, k, j])
-                start(mid.at[p, 1, k, j], product_homes.at[p, 1, j, when],
+                start(mid.at[p, 1, k, j], (s_homes, r_homes)[p].at[1, j, when],
                       send2.at[p, 1, k, j], recv2.at[p, 1, j, when],
                       me.at(me.z, k // 2, k % 2, me.core))
 
@@ -339,6 +326,14 @@
 
     right_product()
     send_products(1)
+
+    before, after, opposite = (me.x + 3) % 4, (me.x + 1) % 4, (me.x + 2) % 4
+    relays = []
+    for slot in range(2):
+        landed(hits.at[slot, before], ring_recv.at[0, slot])
+        relays.append(remote(hits.at[slot, before], hits.at[slot, before], relay_send.at[slot],
+                             relay_recv.at[slot], me.right))
+        relays[-1].start()
 
     halos = []
     parts = ((0, 4), (1, 2))
@@ -387,11 +382,11 @@
 
     for slot in range(2):
         for t in range(6):
-            landed(product_homes.at[0, slot, t // 4, t % 4], recv2.at[0, slot, t // 4, t % 4])
+            landed(s_homes.at[slot, t // 4, t % 4], recv2.at[0, slot, t // 4, t % 4])
         for part, count in parts:
             halos.append(remote(
-                product_homes.at[0, slot, part, pl.ds(0, count)],
-                product_homes.at[0, slot, 4 + part, pl.ds(0, count)],
+                s_homes.at[slot, part, pl.ds(0, count)],
+                s_homes.at[slot, 4 + part, pl.ds(0, count)],
                 halo_send.at[slot, part], halo_recv.at[slot, part], me.left,
             ))
             halos[-1].start()
@@ -421,28 +416,44 @@
 
     for slot in range(2):
         for t in range(6, 16):
-            landed(product_homes.at[0, slot, t // 4, t % 4], recv2.at[0, slot, t // 4, t % 4])
+            landed(s_homes.at[slot, t // 4, t % 4], recv2.at[0, slot, t // 4, t % 4])
+        for part, count in parts:
+            landed(s_homes.at[slot, 4 + part, pl.ds(0, count)], halo_recv.at[slot, part])
+
+    def product_sums_of(first, sums):
+        @pl.loop(0, SPAN)
+        def _(t):
+            totals = [[jnp.zeros((1, BLK), f32) for _ in range(2)] for _ in range(3)]
+            for slot in range(2):
+                one = first(slot, t)
+                for k in range(3):
+                    u = t + seps[k]
+                    two = [s_homes[slot, u // 4, u % 4, c].astype(f32) for c in range(2)]
+                    totals[k] = [a + b for a, b in zip(totals[k], pair_sums(one, two))]
+            for k in range(3):
+                sums[3 * t + k] = jnp.concatenate(totals[k], axis=0)
+
+    product_sums_of(lambda slot, t: [weights[slot, t, c].astype(f32) for c in range(2)], noise_sums)
+
+    for slot in range(2):
         for t in range(16):
-            landed(product_homes.at[1, slot, t // 4, t % 4], recv2.at[1, slot, t // 4, t % 4])
-        for part, count in parts:
-            landed(product_homes.at[0, slot, 4 + part, pl.ds(0, count)], halo_recv.at[slot, part])
-
-    @pl.loop(0, SPAN)
-    def _(t):
-        totals = [[jnp.zeros((1, BLK), f32) for _ in range(4)] for _ in range(3)]
-        for slot in range(2):
-            rt = [product_homes[1, slot, t // 4, t % 4, c].astype(f32) for c in range(2)]
-            w = [weights[slot, t, c].astype(f32) for c in range(2)]
-            for k in range(3):
-                u = t + seps[k]
-                s = [product_homes[0, slot, u // 4, u % 4, c].astype(f32) for c in range(2)]
-                new = pair_sums(rt, s) + pair_sums(w, s)
-                totals[k] = [a + b for a, b in zip(totals[k], new)]
-        for k in range(3):
-            product_sums[3 * t + k] = jnp.concatenate(totals[k], axis=0)
-
-    out[:, 0:4] = jnp.sum(box_sums[...], axis=-1)
-    out[:, 4:8] = jnp.sum(product_sums[...], axis=-1)
+            landed(r_homes.at[slot, t // 4, t % 4], recv2.at[1, slot, t // 4, t % 4])
+    product_sums_of(
+        lambda slot, t: [r_homes[slot, t // 4, t % 4, c].astype(f32) for c in range(2)], cross_sums
+    )
+
+    sums = [(0, 4, box_sums), (4, 6, cross_sums), (6, 8, noise_sums)]
+    for start_at, stop_at, values in sums:
+        reduced = jnp.sum(values[...], axis=-1)
+        for q in range(8):
+            tiles[q, 0:6, start_at:stop_at] = reduced[6 * q:6 * q + 6]
+    mine = 4 * (me.tm % 8) + me.mode
+    for n in range(32):
+        start(tiles.at[n // 4], gather.at[mine], sum_send.at[n], sum_recv.at[mine],
+              (8 * me.x + n // 4, n % 4))
+    for n in range(32):
+        landed(gather.at[n], sum_recv.at[n])
+    out[...] = jnp.sum(gather[...], axis=0)
 
     for copy in assembly + forwards + ring + relays + halos:
         copy.wait_send()
@@ -454,31 +465,6 @@
             @pl.when(me.lo == only)
             def _():
                 sent(me, *copy)
-
-
-def reduce(part, out, gather, send, recv):
-    me = Place()
-    barrier = pltpu.get_barrier_semaphore()
-    base = 8 * me.x
-    mine = 4 * (me.tm % 8) + me.mode
-    others = [(base + n // 4, n % 4) for n in range(32)]
-    for n in range(32):
-        @pl.when(mine != n)
-        def _():
-            pl.semaphore_signal(barrier, inc=1, device_id=others[n], device_id_type=MESH)
-    pl.semaphore_wait(barrier, 31)
-    copies = [(part.at[n // 4], gather.at[mine], send.at[n], recv.at[mine], others[n])
-              for n in range(32)]
-    for copy in copies:
-        send_or_keep(me, *copy)
-    for n in range(32):
-        landed(gather.at[n], recv.at[n])
-    total = jnp.sum(gather[...], axis=0)
-    out[...] = total
-    out[0:1] = total[0:1] * total[2:3] - total[1:2] * total[3:4]
-    out[1:2] = total[0:1] * total[3:4] + total[1:2] * total[2:3]
-    for copy in copies:
-        sent(me, *copy)
 
 
 def params(ident):
@@ -504,9 +490,9 @@
     smem = pl.BlockSpec(memory_space=pltpu.SMEM)
     vmem = pl.BlockSpec(memory_space=pltpu.VMEM)
     dims = lambda *shape: pltpu.VMEM(shape, bf16)
-    part = pl.pallas_call(
+    total = pl.pallas_call(
         contract,
-        out_shape=jax.ShapeDtypeStruct((3 * SPAN, 8), f32),
+        out_shape=jax.ShapeDtypeStruct((8, BLK), f32),
         in_specs=[smem, smem, any_spec, any_spec],
         out_specs=vmem,
         scratch_shapes=[
@@ -516,14 +502,18 @@
             dims(2, 4, 2, 2, BLK, BLK),
             dims(2, 4, 8, 2, BLK, BLK),
             dims(2, 2, 4, 4, 2, BLK, BLK),
-            dims(2, 2, 6, 4, 2, BLK, BLK),
+            dims(2, 6, 4, 2, BLK, BLK),
+            dims(2, 4, 4, 2, BLK, BLK),
             dims(4, 4, 5, 64, BLK),
             dims(2, 4, 4, 2, 5, 64, BLK),
             dims(2, 2 * BLK, 2048),
             dims(16, 2048),
             dims(2, SPAN, 2, BLK, BLK),
             pltpu.VMEM((3 * SPAN, 4, BLK), f32),
-            pltpu.VMEM((3 * SPAN, 4, BLK), f32),
+            pltpu.VMEM((3 * SPAN, 2, BLK), f32),
+            pltpu.VMEM((3 * SPAN, 2, BLK), f32),
+            pltpu.VMEM((8, 8, BLK), f32),
+            pltpu.VMEM((32, 8, BLK), f32),
             dma((2,)), dma((2,)), dma((2,)), dma((2,)),
             dma((2, 2, 4)), dma((4, 4)), dma((4, 4)), dma((2, 4, 2)),
             dma((2, 2)), dma((2, 2)), dma((2,)), dma((2,)),
@@ -531,22 +521,20 @@
             dma((4, 2)), dma((2, 4)), dma((2, 4)), dma((2, 4)), dma((2, 4, 4)),
             dma((2, 4, 2, 4)), dma((2, 2, 4, 4)), dma((2, 2, 4, 4)), dma((2, 2, 4, 4)),
             dma((2, 2)), dma((2, 2)), dma((2, 2)), dma((2, 2)),
+            dma((32,)), dma((32,)),
         ],
         compiler_params=params(0),
         name="contract",
     )(mom_index, separations, fields, noise)
-    part = jnp.pad(part.reshape(8, 6, 8).transpose(0, 2, 1), ((0, 0), (0, 0), (0, BLK - 6)))
-    total = pl.pallas_call(
-        reduce,
-        out_shape=jax.ShapeDtypeStruct((8, BLK), f32),
-        in_specs=[vmem],
-        out_specs=vmem,
-        scratch_shapes=[pltpu.VMEM((32, 8, BLK), f32), dma((32,)), dma((32,))],
-        compiler_params=params(2),
-        name="reduce",
-    )(part)
-    table = total[:, :6].T.reshape(2, 3, 8)
-    return table[..., 0:2], table[..., 4:6], table[..., 6:8]
+    mine = total[:6, :8].reshape(2, 3, 8)
+    box = jnp.stack(
+        [
+            mine[..., 0] * mine[..., 2] - mine[..., 1] * mine[..., 3],
+            mine[..., 0] * mine[..., 3] + mine[..., 1] * mine[..., 2],
+        ],
+        axis=-1,
+    )
+    return box, mine[..., 4:6], mine[..., 6:8]
 
 
 def solution(mesh):

time: 223 us -> 198 us (0.89)
  Pallas kernels: 209 us -> 186 us
    pallas_call x2 -> x1, Pallas kernels: 209 us -> 186 us  [on_device(): pl.pallas_call(contract, out_shape=jax.ShapeDtypeStruct((8, BLK), f32), i...]
where the time goes in v4:
time: 198 us
  Pallas kernels  186 us (94%)
  other arithmetic  6.77 us (3%)
  local copies, waits for them, and re-layouts  4.46 us (2%)
    pallas_call x1, Pallas kernels, on_device(): pl.pallas_call(contract, out_shape=jax.ShapeDtypeStruct((8, BLK), f32), i...  186 us
    transpose x1, other arithmetic, on_device(): fields = fields.transpose(1, 0, 2, 3, 4)  4.86 us

profile of v4, /device:TPU:1, one launch (start us, length us, event | category | flops | bytes accessed | tf_op | source)
XLA Modules:
  0.0 197.8 jit_solution(2808883544652053566)
XLA Ops:
  0.6 0.0 copy-start
  0.6 0.7 convert_element_type.11
  1.4 0.7 copy.16
  2.0 0.1 broadcast_in_dim.2
  2.2 0.0 copy-done
  2.2 0.1 constant_dynamic-slice_fusion
  2.3 1.1 pad_maximum_fusion
  3.3 0.1 reshape.18
  3.4 0.7 copy.26
  4.1 4.9 %fusion.fields = bf16[2,2,2,256,1024]{4,3,2,1,0:T(8,128)(2,1)} fusion(bf16[2,2,2,256,1024]{4,3,2,1,0:T(8,128)(2,1)} %param.7, f32[2,2,256]{2,0,1:T(2,128)S(1)} %copy.16), kind=kLoop, calls=%fused_computation.1 | loop fusion | flops 6291456 | bytes 8392704 | tf_op jit(solution)/shard_map/transpose | solution.py:481
  9.0 185.9 %contract.1 = f32[8,128]{1,0:T(8,128)} custom-call(s32[4]{0:T(128)} %mom.1, s32[3]{0:T(128)} %seps.1, bf16[2,2,2,256,1024]{4,3,2,1,0:T(8,128)(2,1)} %fusion.fields, bf16[2,5,64,128]{3,2,1,0:T(8,128)(2,1)} %bitcast.6), custom_call_target="tpu_custom_call" | custom-call | tf_op jit(solution)/shard_map/contract/pallas_call | solution.py:493
  194.9 0.7 reshape.17
  195.6 0.1 fusion.1
  195.7 0.7 copy.21
  196.3 0.7 copy.20
  197.0 0.1 multiply_subtract_fusion
  197.1 0.1 pad_maximum_fusion.1
  197.1 0.7 copy.19
Async XLA Ops:
  0.6 1.5 copy-start

commit v5 on v4

v5 whole, which is shorter than its diff:
```python
import jax
import jax.numpy as jnp
from jax import lax
from jax.experimental import pallas as pl
from jax.experimental.pallas import tpu as pltpu
from jax.sharding import PartitionSpec as P

MESH = pl.DeviceIdType.MESH
ANY = pl.ANY
BLK = 128
SPAN = 16
VMEM_LIMIT = 56 * 1024 * 1024


def home(i, half, e, same):
    if same:
        if e == 0:
            unit, slot = i % 2, i // 2
        elif e == 1:
            unit, slot = 4 + i, 0
        elif e == 2:
            unit, slot = 2 + i % 2, i // 2
        else:
            unit, slot = 4 + (i + 3) % 4, 1
        return unit // 2, 0, half, unit % 2, slot, 4 * half + (i + e) % 4
    upper, lower = i + half * (e - i), e + half * (i - e)
    return upper, 1, (i + e) % 2, lower // 2, half, 4 * (1 - half) + e


def blocks_of(z, lo, hi, core):
    if z < 2:
        near = (core, core + 2)
    elif z == 2:
        near = (core, core + 1)
    else:
        near = (2 + core, (3 + core) % 4)
    far = (z, 4 + 2 * core + (hi + z) % 2)
    return tuple(4 * hi * (1 - lo) + n + lo * (f - n) for n, f in zip(near, far))


class Place:
    def __init__(self):
        self.tm = lax.axis_index("tm")
        self.mode = lax.axis_index("mode")
        self.x, self.z, self.lo = self.tm // 8, (self.tm // 2) % 4, self.tm % 2
        self.hi, self.core = self.mode // 2, self.mode % 2
        self.right = ((self.tm + 8) % 32, self.mode)
        self.left = ((self.tm + 24) % 32, self.mode)

    def at(self, z, lo, hi, core):
        return (8 * self.x + 2 * z + lo, 2 * hi + core)

    def is_here(self, device):
        return jnp.logical_and(device[0] == self.tm, device[1] == self.mode)


def greet(place):
    barrier = pltpu.get_barrier_semaphore()

    def signal(device):
        pl.semaphore_signal(barrier, inc=1, device_id=device, device_id_type=MESH)

    for n in range(32):
        device = (8 * place.x + n // 4, n % 4)

        @pl.when(jnp.logical_not(place.is_here(device)))
        def _():
            signal(device)

    signal(place.right)
    signal(place.left)
    pl.semaphore_wait(barrier, 33)


def remote(src, dst, send, recv, device):
    return pltpu.make_async_remote_copy(
        src_ref=src, dst_ref=dst, send_sem=send, recv_sem=recv,
        device_id=device, device_id_type=MESH,
    )


def send_or_keep(place, src, dst, send, recv, device):
    here = place.is_here(device)

    @pl.when(jnp.logical_not(here))
    def _():
        remote(src, dst, send, recv, device).start()

    @pl.when(here)
    def _():
        pltpu.make_async_copy(src, dst, recv).start()


def sent(place, src, dst, send, recv, device):
    @pl.when(jnp.logical_not(place.is_here(device)))
    def _():
        remote(src, dst, send, recv, device).wait_send()


def landed(ref, sem):
    pltpu.make_async_copy(ref, ref, sem).wait()


def pair_sums(one, two):
    real = one[0] * two[0] - one[1] * two[1]
    imag = one[0] * two[1] + one[1] * two[0]
    return [jnp.sum(value, axis=0, keepdims=True) for value in (real, imag)]


def contract(
    mom, seps, codes, scales, left, right, ids, out,
    fields, whole, homes, field_tail, mid_y, mid_z, products, mid, s_homes, s_tail, r_homes,
    mid_left, mid_right, mid_ids, hits_left, hits_right, hits_ids,
    left_t, source, weights, box_sums, cross_sums, noise_sums, tiles, gather,
    code_sem, asm_send, asm_recv, fwd_send, fwd_recv,
    left_send, left_z_send, left_z_recv, left_y_send, left_recv,
    id_send, id_z_send, id_z_recv, id_y_send, id_recv,
    right_z_send, right_z_recv, right_y_send, right_recv,
    ring_send, ring_recv, relay_send, relay_recv,
    near_send, cross_z_send, cross_z_recv, cross_y_send,
    whole_z_send, whole_y_send, whole_y_recv, whole_pass_send, home_recv,
    send1, recv1, send2, recv2,
    field_send, field_recv, halo_send, halo_recv, keep, sum_send, sum_recv,
):
    f32, bf16 = jnp.float32, jnp.bfloat16
    me = Place()
    loads = [pltpu.make_async_copy(codes.at[:, s], fields.at[:, s], code_sem.at[s])
             for s in range(2)]
    for copy in loads:
        copy.start()
    tiles[...] = jnp.zeros_like(tiles)
    greet(me)
    flip = me.tm + 1 - 2 * me.lo
    when = 2 * (1 - me.lo) + me.hi
    sends = []

    def start(*copy, only=None):
        sends.append((copy, only))
        if only is None:
            send_or_keep(me, *copy)
        else:

            @pl.when(me.lo == only)
            def _():
                send_or_keep(me, *copy)

    def landed_if(only, ref, sem):
        @pl.when(me.lo == only)
        def _():
            landed(ref, sem)

    def tile(n):
        return pl.ds(n * BLK if isinstance(n, int) else pl.multiple_of(n * BLK, BLK), BLK)

    def rows_of(block):
        return whole.at[:, :, pl.ds(pl.multiple_of(block * 256, 256), 256), :]

    for z in range(4):
        for slot in range(2):
            hi = me.hi + slot * (1 - 2 * me.hi)
            far = blocks_of(z, 1 - me.lo, hi, me.core)[slot]
            start(left.at[far], mid_left.at[slot, me.z], left_z_send.at[z, slot],
                  left_z_recv.at[slot, me.z], me.at(z, me.lo, me.hi, me.core))
        start(ids, mid_ids.at[me.z], id_z_send.at[z], id_z_recv.at[me.z],
              me.at(z, me.lo, me.hi, me.core))
    for a in range(2):
        for same in (False, True):
            for e in range(4):
                z, lo, hi, core, slot, col = home(2 * me.core + a, me.hi, e, same)
                group = slot if same else 2 + hi
                start(right.at[a], mid_right.at[group, me.z], right_z_send.at[a, int(same), e],
                      right_z_recv.at[group, me.z], me.at(z, me.lo, me.hi, core))

    assembly = []
    for s in range(2):
        loads[s].wait()
        for m in range(2):
            column = jnp.broadcast_to(scales[m, s:s + 1, :], (BLK, 256)).T

            @pl.loop(0, 8)
            def _(n):
                for c in range(2):
                    value = fields[m, s, c, :, tile(n)].astype(f32) * column
                    fields[m, s, c, :, tile(n)] = value.astype(bf16)

        assembly.append(remote(fields.at[:, s], rows_of(me.mode), asm_send.at[s],
                               asm_recv.at[me.hi], (flip, 2 * s + me.core)))
        assembly[-1].start()

    for a in range(2):
        row = 2 * me.core + a
        for e in range(4):
            z, _, hi, core, slot, col = home(row, me.hi, e, True)
            far = home(row, me.hi, e, False)

            def pick(one, two):
                return one + me.lo * (two - one)

            s, group = pick(1 - far[2], 1 - me.hi), pick(far[2], slot)
            start(fields.at[:, s, :, tile(a), tile(pick(far[5], col))], mid_y.at[group, me.z],
                  cross_z_send.at[a, e], cross_z_recv.at[group, me.z],
                  me.at(pick(far[0], z), me.lo, me.hi, pick(far[3], core)))
        for s in range(2):
            for e in range(4):
                z, _, hi, core, slot, col = home(row, me.hi, e, True)
                start(fields.at[:, s, :, tile(a), tile(col)], homes.at[slot, 4 * me.z + s],
                      near_send.at[s, a, e], home_recv.at[slot, 4 * me.z + s],
                      me.at(z, 0, me.hi, core), only=0)
            for b in range(2):
                other = 2 * b + (me.hi + a) % 2
                z, _, hi, core, slot, col = home(row, me.hi, other, False)
                start(fields.at[:, s, :, tile(a), tile(col)], homes.at[slot, 4 * me.z + 2 + s],
                      near_send.at[s, a, 4 + b], home_recv.at[slot, 4 * me.z + 2 + s],
                      me.at(z, 1, me.hi, core), only=1)

    for z in range(4):
        for slot in range(2):
            hi = me.hi + slot * (1 - 2 * me.hi)
            landed(mid_left.at[slot, z], left_z_recv.at[slot, z])
            start(mid_left.at[slot, z], hits_left.at[slot, me.x, z, me.lo],
                  left_y_send.at[slot, z], left_recv.at[slot, z, me.lo],
                  me.at(me.z, 1 - me.lo, hi, me.core))
        landed(mid_ids.at[z], id_z_recv.at[z])
        start(mid_ids.at[z], hits_ids.at[me.x, z, me.lo], id_y_send.at[z],
              id_recv.at[z, me.lo], me.at(me.z, 1 - me.lo, me.hi, me.core))
        for group in range(4):
            if group < 2:
                slot, device = group, me.at(me.z, 0, me.hi, me.core)
            else:
                slot, device = me.hi, me.at(me.z, 1, group - 2, me.core)
            landed(mid_right.at[group, z], right_z_recv.at[group, z])
            start(mid_right.at[group, z], hits_right.at[slot, me.x, z, me.lo],
                  right_y_send.at[group, z], right_recv.at[slot, z, me.lo], device)
        for slot in range(2):
            near = blocks_of(z, me.lo, me.hi, me.core)[slot]
            start(left.at[near], hits_left.at[slot, me.x, me.z, me.lo], left_send.at[z, slot],
                  left_recv.at[slot, me.z, me.lo], me.at(z, me.lo, me.hi, me.core))
        start(ids, hits_ids.at[me.x, me.z, me.lo], id_send.at[z], id_recv.at[me.z, me.lo],
              me.at(z, me.lo, me.hi, me.core))

    ring = []

    def start_ring():
        for z in range(4):
            for lo in range(2):
                for slot in range(2):
                    landed(hits_left.at[slot, me.x, z, lo], left_recv.at[slot, z, lo])
                    landed(hits_right.at[slot, me.x, z, lo], right_recv.at[slot, z, lo])
                landed(hits_ids.at[me.x, z, lo], id_recv.at[z, lo])
        own = [hits_left.at[:, me.x], hits_right.at[:, me.x], hits_ids.at[me.x]]
        for n, ref in enumerate(own):
            ring.append(remote(ref, ref, ring_send.at[0, n], ring_recv.at[0, n], me.right))
        for n, ref in enumerate(own):
            ring.append(remote(ref, ref, ring_send.at[1, n], ring_recv.at[1, n], me.left))
        for copy in ring:
            copy.start()

    before, after, opposite = (me.x + 3) % 4, (me.x + 1) % 4, (me.x + 2) % 4
    relays = []

    def relay():
        held = [hits_left.at[:, before], hits_right.at[:, before], hits_ids.at[before]]
        for n, ref in enumerate(held):
            landed(ref, ring_recv.at[0, n])
            relays.append(remote(ref, ref, relay_send.at[n], relay_recv.at[n], me.right))
            relays[-1].start()

    start_ring()

    forwards = []
    for h in range(2):
        block = rows_of(2 * h + me.core)
        landed(block, asm_recv.at[h])
        forwards.append(remote(block, block, fwd_send.at[h], fwd_recv.at[h],
                               (me.tm, me.mode + 1 - 2 * me.core)))
        forwards[-1].start()

    for z in range(4):
        for group in range(2):
            landed(mid_y.at[group, z], cross_z_recv.at[group, z])
            lo, hi = 1 - me.lo, group + me.lo * (me.hi - group)
            slot = me.hi + me.lo * (group - me.hi)
            t = 4 * z + 2 * me.lo + (1 - group) + me.lo * (group - me.hi)
            start(mid_y.at[group, z], homes.at[slot, t], cross_y_send.at[group, z],
                  home_recv.at[slot, t], me.at(me.z, lo, hi, me.core))

    def serve(only, slot, t):
        landed_if(only, homes.at[slot, t], home_recv.at[slot, t])
        start(homes.at[slot, t], field_tail.at[slot, 6 + t], field_send.at[slot, t],
              field_recv.at[slot, t], me.left, only=only)

    for t in (0, 1, 4, 5):
        for slot in range(2):
            serve(0, slot, t)
    for t in (2, 3):
        serve(1, me.hi, t)

    for h in range(2):
        landed(rows_of(2 * h + 1 - me.core), fwd_recv.at[h])
    for hi in range(2):
        for z in range(4):
            pair = blocks_of(z, 1, hi, me.core)
            row, col = pair[1 - hi], pair[hi]
            start(whole.at[:, :, tile(row), tile(col)], mid_z.at[me.hi, z],
                  whole_y_send.at[hi, z], whole_y_recv.at[me.hi, z],
                  me.at(me.z, 1, hi, me.core), only=0)
    for z in range(4):
        pair = blocks_of(z, me.lo, me.hi, me.core)
        for slot in range(2):
            row, col = pair[slot], pair[1 - slot]
            if z == 0:
                col = col + (1 - me.lo) * (row - col)
            start(whole.at[:, :, tile(row), tile(col)], homes.at[slot, 4 * me.z + when],
                  whole_z_send.at[z, slot], home_recv.at[slot, 4 * me.z + when],
                  me.at(z, me.lo, me.hi, me.core))

    base = pl.multiple_of(me.core * 512, 512)
    m1, m2, m3, m4 = (mom[i] for i in range(4))

    def cdot(ar, ai, br, bi):
        def dot(a, b):
            return jnp.dot(a, b, preferred_element_type=f32)

        return dot(ar, br) - dot(ai, bi), dot(ar, bi) + dot(ai, br)

    def product_s():
        @pl.loop(0, 4)
        def _(pair):
            cols = pl.ds(pl.multiple_of(pair * 256, 256), 256)
            rows = pl.ds(base, 512)
            parts = cdot(whole[m2, 0, rows, :], whole[m2, 1, rows, :],
                         whole[m3, 0, :, cols], whole[m3, 1, :, cols])
            for c in range(2):
                for a in range(4):
                    for b in range(2):
                        piece = parts[c][a * BLK:(a + 1) * BLK, b * BLK:(b + 1) * BLK]
                        products[0, a, 2 * pair + b, c] = piece.astype(bf16)

    def product_r():
        @pl.loop(0, 4)
        def _(step):
            pair, half = step // 2, step % 2
            cols = pl.ds(pl.multiple_of(base + pair * 256, 256), 256)
            rows = pl.ds(pl.multiple_of(half * 512, 512), 512)
            parts = cdot(whole[m4, 0, rows, :], whole[m4, 1, rows, :],
                         whole[m1, 0, :, cols], whole[m1, 1, :, cols])
            for c in range(2):
                for a in range(2):
                    for b in range(4):
                        piece = parts[c][b * BLK:(b + 1) * BLK, a * BLK:(a + 1) * BLK]
                        products[1, 2 * pair + a, 4 * half + b, c] = piece.T.astype(bf16)

    def send_products(p):
        for i in range(4):
            for same in (False, True):
                for e in range(4):
                    z, lo, hi, core, slot, col = home(i, me.core, e, same)

                    def either(one, two):
                        return one + slot * (two - one)

                    device = me.at(either(me.z, z), either(lo, me.lo), either(hi, me.hi), core)
                    at = (p, slot, either(z, 2 * lo + hi), either(when, me.z))
                    start(products.at[p, i, col], mid.at[at], send1.at[p, i, int(same), e],
                          recv1.at[at], device)

    def pass_on(p):
        ref = (s_homes, r_homes)[p]
        for j in range(4):
            for k in range(4):
                landed(mid.at[p, 0, k, j], recv1.at[p, 0, k, j])
                start(mid.at[p, 0, k, j], ref.at[0, 4 * me.z + j],
                      send2.at[p, 0, k, j], recv2.at[p, 0, 4 * me.z + j],
                      me.at(k, me.lo, me.hi, me.core))
                landed(mid.at[p, 1, k, j], recv1.at[p, 1, k, j])
                start(mid.at[p, 1, k, j], ref.at[1, 4 * j + when],
                      send2.at[p, 1, k, j], recv2.at[p, 1, 4 * j + when],
                      me.at(me.z, k // 2, k % 2, me.core))

    def pass_fields():
        for hi in range(2):
            for z in range(4):
                landed_if(1, mid_z.at[hi, z], whole_y_recv.at[hi, z])
                start(mid_z.at[hi, z], homes.at[1 - me.hi, 4 * me.z + 2 + hi],
                      whole_pass_send.at[hi, z], home_recv.at[1 - me.hi, 4 * me.z + 2 + hi],
                      me.at(z, 1, me.hi, me.core), only=1)

    def serve_rest():
        for t in (2, 3):
            for slot in range(2):
                serve(0, slot, t)
        for t in (0, 1, 4, 5):
            serve(1, me.hi, t)
        for t in range(6):
            serve(1, 1 - me.hi, t)

    kept = []

    def fields_here():
        for slot in range(2):
            for t in range(6, 16):
                landed(homes.at[slot, t], home_recv.at[slot, t])
            kept.append(pltpu.make_async_copy(
                homes.at[slot, pl.ds(10, 6)], field_tail.at[slot, pl.ds(0, 6)], keep.at[0, slot]))
            kept[-1].start()

    def serve_products():
        for slot in range(2):
            for t in range(6):
                landed(s_homes.at[slot, t], recv2.at[0, slot, t])
                start(s_homes.at[slot, t], s_tail.at[slot, 6 + t], halo_send.at[slot, t],
                      halo_recv.at[slot, t], me.left)

    def products_here():
        for slot in range(2):
            for t in range(6, 16):
                landed(s_homes.at[slot, t], recv2.at[0, slot, t])
            kept.append(pltpu.make_async_copy(
                s_homes.at[slot, pl.ds(10, 6)], s_tail.at[slot, pl.ds(0, 6)], keep.at[1, slot]))
            kept[-1].start()

    def left_vectors():
        for role in range(2):
            for c in range(2):

                @pl.loop(0, 16)
                def _(part):
                    block = hits_left[role, part // 4, part % 4, :, c].reshape(BLK, BLK)
                    left_t[role, pl.ds(c * BLK, BLK), tile(part)] = block.T

        lanes = lax.broadcasted_iota(jnp.int32, (16, BLK), 1)

        @pl.loop(0, 16)
        def _(part):
            one, two = (hits_ids[part // 4, part % 4, lo].astype(f32) for lo in range(2))
            source[:, tile(part)] = jnp.where(lanes < 64, one, two)

    diagonal = jnp.logical_and(me.lo == 0, me.z == 0)

    def all_weights():
        @pl.loop(0, SPAN)
        def _(t):
            stamp = (me.x * SPAN + t).astype(f32)
            chosen = (source[:1, :] == stamp).astype(f32).astype(bf16)
            for slot in range(2):
                mate = jnp.where(diagonal, slot, 1 - slot)
                vectors = jnp.concatenate(
                    [hits_right[mate, :, :, :, c].reshape(2048, BLK) for c in range(2)], axis=1
                )
                pieces = jnp.dot(left_t[slot] * chosen, vectors, preferred_element_type=f32)
                weights[slot, t, 0] = (pieces[:BLK, :BLK] - pieces[BLK:, BLK:]).astype(bf16)
                weights[slot, t, 1] = (pieces[:BLK, BLK:] + pieces[BLK:, :BLK]).astype(bf16)

    def box(begin, end, later, shift):
        @pl.loop(begin, end)
        def _(t):
            totals = [[jnp.zeros((1, BLK), f32) for _ in range(4)] for _ in range(3)]
            for slot in range(2):
                mate = jnp.where(diagonal, slot, 1 - slot)
                p1 = [homes[slot, t, m1, c].astype(f32).T for c in range(2)]
                p4 = [homes[slot, t, m4, c].astype(f32).T for c in range(2)]
                for k in range(3):
                    u = t + seps[k] - shift
                    p2 = [later[mate, u, m2, c].astype(f32) for c in range(2)]
                    p3 = [later[mate, u, m3, c].astype(f32) for c in range(2)]
                    new = pair_sums(p1, p2) + pair_sums(p4, p3)
                    totals[k] = [a + b for a, b in zip(totals[k], new)]
            for k in range(3):
                box_sums[3 * t + k] = jnp.concatenate(totals[k], axis=0)

    def product_sums(begin, end, later, shift, first, sums):
        @pl.loop(begin, end)
        def _(t):
            totals = [[jnp.zeros((1, BLK), f32) for _ in range(2)] for _ in range(3)]
            for slot in range(2):
                one = [first[slot, t, c].astype(f32) for c in range(2)]
                for k in range(3):
                    u = t + seps[k] - shift
                    two = [later[slot, u, c].astype(f32) for c in range(2)]
                    totals[k] = [a + b for a, b in zip(totals[k], pair_sums(one, two))]
            for k in range(3):
                sums[3 * t + k] = jnp.concatenate(totals[k], axis=0)

    def to_tiles(begin, end, sums):
        reduced = jnp.sum(sums[...], axis=-1)
        for q in range(8):
            tiles[q, 0:6, begin:end] = reduced[6 * q:6 * q + 6]

    product_s()
    send_products(0)
    product_r()
    pass_fields()
    relay()
    serve_rest()
    pass_on(0)
    send_products(1)
    fields_here()
    box(0, 10, homes, 0)
    ring_refs = [hits_left.at[:, after], hits_right.at[:, after], hits_ids.at[after]]
    relay_refs = [hits_left.at[:, opposite], hits_right.at[:, opposite], hits_ids.at[opposite]]
    for n in range(3):
        landed(ring_refs[n], ring_recv.at[1, n])
        landed(relay_refs[n], relay_recv.at[n])
    left_vectors()
    serve_products()
    pass_on(1)
    all_weights()
    for copy in kept:
        copy.wait()
    for slot in range(2):
        for t in range(6):
            landed(field_tail.at[slot, 6 + t], field_recv.at[slot, t])
    box(10, 16, field_tail, 10)
    to_tiles(0, 4, box_sums)
    products_here()
    product_sums(0, 10, s_homes, 0, weights, noise_sums)
    for copy in kept[2:]:
        copy.wait()
    for slot in range(2):
        for t in range(6):
            landed(s_tail.at[slot, 6 + t], halo_recv.at[slot, t])
    product_sums(10, 16, s_tail, 10, weights, noise_sums)
    to_tiles(6, 8, noise_sums)
    for slot in range(2):
        for t in range(16):
            landed(r_homes.at[slot, t], recv2.at[1, slot, t])
    product_sums(0, 10, s_homes, 0, r_homes, cross_sums)
    product_sums(10, 16, s_tail, 10, r_homes, cross_sums)
    to_tiles(4, 6, cross_sums)

    mine = 4 * (me.tm % 8) + me.mode
    for n in range(32):
        start(tiles.at[n // 4], gather.at[mine], sum_send.at[n], sum_recv.at[mine],
              (8 * me.x + n // 4, n % 4))
    for n in range(32):
        landed(gather.at[n], sum_recv.at[n])
    out[...] = jnp.sum(gather[...], axis=0)

    for copy in assembly + forwards + ring + relays:
        copy.wait_send()
    for copy, only in sends:
        if only is None:
            sent(me, *copy)
        else:

            @pl.when(me.lo == only)
            def _():
                sent(me, *copy)


def params(ident):
    return pltpu.CompilerParams(
        vmem_limit_bytes=VMEM_LIMIT, collective_id=ident, has_side_effects=True
    )


def on_device(field_codes, scales, mom_index, separations, source_slice, noise_left, noise_right):
    bf16, f32 = jnp.bfloat16, jnp.float32
    dma = pltpu.SemaphoreType.DMA
    blocks = noise_left.reshape(64, 2, 8, BLK).transpose(2, 1, 0, 3)
    own_blocks = noise_right.reshape(64, 2, 2, BLK).transpose(2, 1, 0, 3)
    ids = jnp.broadcast_to(jnp.tile(source_slice.astype(bf16), 2), (16, BLK))

    any_spec = pl.BlockSpec(memory_space=ANY)
    smem = pl.BlockSpec(memory_space=pltpu.SMEM)
    vmem = pl.BlockSpec(memory_space=pltpu.VMEM)
    dims = lambda *shape: pltpu.VMEM(shape, bf16)
    total = pl.pallas_call(
        contract,
        out_shape=jax.ShapeDtypeStruct((8, BLK), f32),
        in_specs=[smem, smem, any_spec, vmem, any_spec, any_spec, any_spec],
        out_specs=vmem,
        scratch_shapes=[
            dims(2, 2, 2, 256, 1024),
            dims(2, 2, 1024, 1024),
            dims(2, 16, 2, 2, BLK, BLK),
            dims(2, 12, 2, 2, BLK, BLK),
            dims(2, 4, 2, 2, BLK, BLK),
            dims(2, 4, 2, 2, BLK, BLK),
            dims(2, 4, 8, 2, BLK, BLK),
            dims(2, 2, 4, 4, 2, BLK, BLK),
            dims(2, 16, 2, BLK, BLK),
            dims(2, 12, 2, BLK, BLK),
            dims(2, 16, 2, BLK, BLK),
            dims(2, 4, 2, 64, BLK),
            dims(4, 4, 2, 64, BLK),
            dims(4, 16, BLK),
            dims(2, 4, 4, 2, 2, 64, BLK),
            dims(2, 4, 4, 2, 2, 64, BLK),
            dims(4, 4, 2, 16, BLK),
            dims(2, 2 * BLK, 2048),
            pltpu.VMEM((16, 2048), f32),
            dims(2, SPAN, 2, BLK, BLK),
            pltpu.VMEM((3 * SPAN, 4, BLK), f32),
            pltpu.VMEM((3 * SPAN, 2, BLK), f32),
            pltpu.VMEM((3 * SPAN, 2, BLK), f32),
            pltpu.VMEM((8, 8, BLK), f32),
            pltpu.VMEM((32, 8, BLK), f32),
            dma((2,)), dma((2,)), dma((2,)), dma((2,)), dma((2,)),
            dma((4, 2)), dma((4, 2)), dma((2, 4)), dma((2, 4)), dma((2, 4, 2)),
            dma((4,)), dma((4,)), dma((4,)), dma((4,)), dma((4, 2)),
            dma((2, 2, 4)), dma((4, 4)), dma((4, 4)), dma((2, 4, 2)),
            dma((2, 3)), dma((2, 3)), dma((3,)), dma((3,)),
            dma((2, 2, 6)), dma((2, 4)), dma((2, 4)), dma((2, 4)),
            dma((4, 2)), dma((2, 4)), dma((2, 4)), dma((2, 4)), dma((2, 16)),
            dma((2, 4, 2, 4)), dma((2, 2, 4, 4)), dma((2, 2, 4, 4)), dma((2, 2, 16)),
            dma((2, 6)), dma((2, 6)), dma((2, 6)), dma((2, 6)), dma((2, 2)),
            dma((32,)), dma((32,)),
        ],
        compiler_params=params(0),
        name="contract",
    )(mom_index, separations, field_codes, scales, blocks, own_blocks, ids)
    mine = total[:6, :8].reshape(2, 3, 8)
    box = jnp.stack(
        [
            mine[..., 0] * mine[..., 2] - mine[..., 1] * mine[..., 3],
            mine[..., 0] * mine[..., 3] + mine[..., 1] * mine[..., 2],
        ],
        axis=-1,
    )
    return box, mine[..., 4:6], mine[..., 6:8]


def solution(mesh):
    in_specs = (
        P(None, "tm", None, "mode", None),
        P(None, "tm", "mode"),
        P(),
        P(),
        P("tm"),
        P("tm", None, None),
        P("tm", None, "mode"),
    )
    out_specs = (P("tm", None, None), P("tm", None, None), P("tm", None, None))
    return jax.shard_map(
        on_device, mesh=mesh, in_specs=in_specs, out_specs=out_specs, check_vma=False
    )
```

time: 198 us -> 178 us (0.90)
  Pallas kernels: 186 us -> 169 us
  other arithmetic: 6.77 us -> 0.81 us
  local copies, waits for them, and re-layouts: 4.46 us -> 6.87 us
    pallas_call x1, Pallas kernels: 186 us -> 169 us  [on_device(): pl.pallas_call(contract, out_shape=jax.ShapeDtypeStruct((8, BLK), f32), i...]
    transpose x1 -> x0, other arithmetic: 4.86 us -> none  [on_device(): fields = fields.transpose(1, 0, 2, 3, 4)]
    reshape x2 -> x4, local copies, waits for them, and re-layouts: 0.79 us -> 3.4 us  [the longest x2 1.88 us: on_device(): blocks = noise_left.reshape(64, 2, 8, BLK).transpose(2, 1, 0, 3)]
where the time goes in v5:
time: 178 us; the launch traced here: 177 us
  Pallas kernels  169 us (95%)
  local copies, waits for them, and re-layouts  6.87 us (4%)
    pallas_call x1, Pallas kernels, on_device(): pl.pallas_call(contract, out_shape=jax.ShapeDtypeStruct((8, BLK), f32), i...  169 us

profile of v5, /device:TPU:1, one launch (start us, length us, event | category | flops | bytes accessed | tf_op | source)
XLA Modules:
  0.0 177.3 jit_solution(17139669628790013594)
XLA Ops:
  0.6 1.1 reshape.19
  1.8 0.8 copy.26
  2.5 0.9 reshape.20
  3.4 0.6 copy.27
  4.0 0.7 convert_element_type.3
  4.7 0.1 tile.10
  4.8 0.6 broadcast_in_dim.3.ids
  5.4 168.9 %contract.1 = f32[8,128]{1,0:T(8,128)} custom-call(s32[4]{0:T(128)} %mom.1, s32[3]{0:T(128)} %seps.1, bf16[2,2,2,256,1024]{4,3,2,1,0:T(8,128)(2,1)} %codes.1, f32[2,2,256]{2,1,0:T(2,128)} %scales.1, bf16[8,2,64,128]{3,2,1,0:T(8,128)(2,1)} %bitcast.7, bf16[2,2,64,128]{3,2,1,0:T(8,128)(2,1)} %bitcast.8, bf16[16,128]{1,0:T(8,128)(2,1)} %broadcast_in_dim.3.ids), custom_call_target="tpu_custom_call" | custom-call | tf_op jit(solution)/shard_map/contract/pallas_call | solution.py:568
  174.3 0.7 reshape.18
  175.0 0.1 multiply_subtract_fusion
  175.1 0.1 pad_maximum_fusion
  175.2 0.7 copy.17
  175.8 0.1 fusion
  175.9 0.7 copy.18
  176.6 0.7 copy.19
  (1 shorter events, 0.0 us)

commit v6 on v5

--- a/solution.py
+++ b/solution.py
@@ -144,6 +144,18 @@
             def _():
                 send_or_keep(me, *copy)
 
+    def all_sent():
+        for copy, only in sends:
+            if only is None:
+                sent(me, *copy)
+            else:
+
+                @pl.when(me.lo == only)
+                def _():
+                    sent(me, *copy)
+
+        sends.clear()
+
     def landed_if(only, ref, sem):
         @pl.when(me.lo == only)
         def _():
@@ -265,8 +277,6 @@
             relays.append(remote(ref, ref, relay_send.at[n], relay_recv.at[n], me.right))
             relays[-1].start()
 
-    start_ring()
-
     forwards = []
     for h in range(2):
         block = rows_of(2 * h + me.core)
@@ -283,6 +293,8 @@
             t = 4 * z + 2 * me.lo + (1 - group) + me.lo * (group - me.hi)
             start(mid_y.at[group, z], homes.at[slot, t], cross_y_send.at[group, z],
                   home_recv.at[slot, t], me.at(me.z, lo, hi, me.core))
+
+    start_ring()
 
     def serve(only, slot, t):
         landed_if(only, homes.at[slot, t], home_recv.at[slot, t])
@@ -521,6 +533,9 @@
             landed(s_tail.at[slot, 6 + t], halo_recv.at[slot, t])
     product_sums(10, 16, s_tail, 10, weights, noise_sums)
     to_tiles(6, 8, noise_sums)
+    for copy in assembly + forwards + ring + relays:
+        copy.wait_send()
+    all_sent()
     for slot in range(2):
         for t in range(16):
             landed(r_homes.at[slot, t], recv2.at[1, slot, t])
@@ -536,16 +551,7 @@
         landed(gather.at[n], sum_recv.at[n])
     out[...] = jnp.sum(gather[...], axis=0)
 
-    for copy in assembly + forwards + ring + relays:
-        copy.wait_send()
-    for copy, only in sends:
-        if only is None:
-            sent(me, *copy)
-        else:
-
-            @pl.when(me.lo == only)
-            def _():
-                sent(me, *copy)
+    all_sent()
 
 
 def params(ident):

time: 178 us -> 170 us (0.955)
  Pallas kernels: 169 us -> 161 us
    pallas_call x1, Pallas kernels: 169 us -> 161 us  [on_device(): pl.pallas_call(contract, out_shape=jax.ShapeDtypeStruct((8, BLK), f32), i...]
where the time goes in v6:
time: 170 us; the launch traced here: 169 us
  Pallas kernels  161 us (95%)
  local copies, waits for them, and re-layouts  6.87 us (4%)
    pallas_call x1, Pallas kernels, on_device(): pl.pallas_call(contract, out_shape=jax.ShapeDtypeStruct((8, BLK), f32), i...  161 us

profile of v6, /device:TPU:1, one launch (start us, length us, event | category | flops | bytes accessed | tf_op | source)
XLA Modules:
  0.0 169.3 jit_solution(17210267843071342959)
XLA Ops:
  0.6 1.1 reshape.19
  1.8 0.8 copy.26
  2.5 0.9 reshape.20
  3.4 0.6 copy.27
  4.0 0.7 convert_element_type.3
  4.7 0.1 tile.10
  4.8 0.6 broadcast_in_dim.3.ids
  5.4 161.0 %contract.1 = f32[8,128]{1,0:T(8,128)} custom-call(s32[4]{0:T(128)} %mom.1, s32[3]{0:T(128)} %seps.1, bf16[2,2,2,256,1024]{4,3,2,1,0:T(8,128)(2,1)} %codes.1, f32[2,2,256]{2,1,0:T(2,128)} %scales.1, bf16[8,2,64,128]{3,2,1,0:T(8,128)(2,1)} %bitcast.7, bf16[2,2,64,128]{3,2,1,0:T(8,128)(2,1)} %bitcast.8, bf16[16,128]{1,0:T(8,128)(2,1)} %broadcast_in_dim.3.ids), custom_call_target="tpu_custom_call" | custom-call | tf_op jit(solution)/shard_map/contract/pallas_call | solution.py:574
  166.4 0.7 reshape.18
  167.0 0.1 multiply_subtract_fusion
  167.1 0.1 pad_maximum_fusion
  167.2 0.7 copy.17
  167.9 0.1 fusion
  167.9 0.7 copy.18
  168.6 0.7 copy.19
  (1 shorter events, 0.0 us)

commit v7 on v6

--- a/solution.py
+++ b/solution.py
@@ -108,10 +108,11 @@
 
 
 def contract(
-    mom, seps, codes, scales, left, right, ids, out,
+    mom, seps, codes, scales, all_left, all_right, all_ids, out,
+    left, right, ids,
     fields, whole, homes, field_tail, mid_y, mid_z, products, mid, s_homes, s_tail, r_homes,
     mid_left, mid_right, mid_ids, hits_left, hits_right, hits_ids,
-    left_t, source, weights, box_sums, cross_sums, noise_sums, tiles, gather,
+    left_t, source, partial, weights, box_sums, cross_sums, noise_sums, tiles, gather,
     code_sem, asm_send, asm_recv, fwd_send, fwd_recv,
     left_send, left_z_send, left_z_recv, left_y_send, left_recv,
     id_send, id_z_send, id_z_recv, id_y_send, id_recv,
@@ -167,6 +168,30 @@
     def rows_of(block):
         return whole.at[:, :, pl.ds(pl.multiple_of(block * 256, 256), 256), :]
 
+    assembly = []
+    for s in range(2):
+        loads[s].wait()
+        for m in range(2):
+            column = jnp.broadcast_to(scales[m, s:s + 1, :], (BLK, 256)).T
+
+            @pl.loop(0, 8)
+            def _(n):
+                for c in range(2):
+                    value = fields[m, s, c, :, tile(n)].astype(f32) * column
+                    fields[m, s, c, :, tile(n)] = value.astype(bf16)
+
+        assembly.append(remote(fields.at[:, s], rows_of(me.mode), asm_send.at[s],
+                               asm_recv.at[me.hi], (flip, 2 * s + me.core)))
+        assembly[-1].start()
+
+    for ref, into, count in ((all_left, left, 8), (all_right, right, 2)):
+        for c in range(2):
+            value = ref[:, c, :]
+            for n in range(count):
+                into[n, c] = value[:, n * BLK:(n + 1) * BLK]
+    row = all_ids[...].astype(f32)
+    ids[...] = jnp.broadcast_to(jnp.concatenate([row, row], axis=1), (16, BLK)).astype(bf16)
+
     for z in range(4):
         for slot in range(2):
             hi = me.hi + slot * (1 - 2 * me.hi)
@@ -182,22 +207,6 @@
                 group = slot if same else 2 + hi
                 start(right.at[a], mid_right.at[group, me.z], right_z_send.at[a, int(same), e],
                       right_z_recv.at[group, me.z], me.at(z, me.lo, me.hi, core))
-
-    assembly = []
-    for s in range(2):
-        loads[s].wait()
-        for m in range(2):
-            column = jnp.broadcast_to(scales[m, s:s + 1, :], (BLK, 256)).T
-
-            @pl.loop(0, 8)
-            def _(n):
-                for c in range(2):
-                    value = fields[m, s, c, :, tile(n)].astype(f32) * column
-                    fields[m, s, c, :, tile(n)] = value.astype(bf16)
-
-        assembly.append(remote(fields.at[:, s], rows_of(me.mode), asm_send.at[s],
-                               asm_recv.at[me.hi], (flip, 2 * s + me.core)))
-        assembly[-1].start()
 
     for a in range(2):
         row = 2 * me.core + a
@@ -277,6 +286,17 @@
             relays.append(remote(ref, ref, relay_send.at[n], relay_recv.at[n], me.right))
             relays[-1].start()
 
+    def serve(only, slot, t):
+        landed_if(only, homes.at[slot, t], home_recv.at[slot, t])
+        start(homes.at[slot, t], field_tail.at[slot, 6 + t], field_send.at[slot, t],
+              field_recv.at[slot, t], me.left, only=only)
+
+    for t in (0, 1, 4, 5):
+        for slot in range(2):
+            serve(0, slot, t)
+    for t in (2, 3):
+        serve(1, me.hi, t)
+
     forwards = []
     for h in range(2):
         block = rows_of(2 * h + me.core)
@@ -295,17 +315,6 @@
                   home_recv.at[slot, t], me.at(me.z, lo, hi, me.core))
 
     start_ring()
-
-    def serve(only, slot, t):
-        landed_if(only, homes.at[slot, t], home_recv.at[slot, t])
-        start(homes.at[slot, t], field_tail.at[slot, 6 + t], field_send.at[slot, t],
-              field_recv.at[slot, t], me.left, only=only)
-
-    for t in (0, 1, 4, 5):
-        for slot in range(2):
-            serve(0, slot, t)
-    for t in (2, 3):
-        serve(1, me.hi, t)
 
     for h in range(2):
         landed(rows_of(2 * h + 1 - me.core), fwd_recv.at[h])
@@ -431,37 +440,49 @@
                 s_homes.at[slot, pl.ds(10, 6)], s_tail.at[slot, pl.ds(0, 6)], keep.at[1, slot]))
             kept[-1].start()
 
-    def left_vectors():
-        for role in range(2):
-            for c in range(2):
-
-                @pl.loop(0, 16)
-                def _(part):
-                    block = hits_left[role, part // 4, part % 4, :, c].reshape(BLK, BLK)
-                    left_t[role, pl.ds(c * BLK, BLK), tile(part)] = block.T
-
-        lanes = lax.broadcasted_iota(jnp.int32, (16, BLK), 1)
-
-        @pl.loop(0, 16)
-        def _(part):
-            one, two = (hits_ids[part // 4, part % 4, lo].astype(f32) for lo in range(2))
-            source[:, tile(part)] = jnp.where(lanes < 64, one, two)
+    lanes = lax.broadcasted_iota(jnp.int32, (16, BLK), 1)
+    order = (me.x, before, after, opposite)
+
+    def left_vectors(planes):
+        for n in planes:
+            for role in range(2):
+                for c in range(2):
+
+                    @pl.loop(0, 4)
+                    def _(part):
+                        block = hits_left[role, order[n], part, :, c].reshape(BLK, BLK)
+                        left_t[role, pl.ds(c * BLK, BLK), tile(4 * n + part)] = block.T
+
+            @pl.loop(0, 4)
+            def _(part):
+                one, two = (hits_ids[order[n], part, lo].astype(f32) for lo in range(2))
+                source[:, tile(4 * n + part)] = jnp.where(lanes < 64, one, two)
 
     diagonal = jnp.logical_and(me.lo == 0, me.z == 0)
 
-    def all_weights():
+    def add_weights(planes, first):
+        span = slice(512 * planes[0], 512 * (planes[-1] + 1))
+
         @pl.loop(0, SPAN)
         def _(t):
             stamp = (me.x * SPAN + t).astype(f32)
-            chosen = (source[:1, :] == stamp).astype(f32).astype(bf16)
+            chosen = (source[:1, span] == stamp).astype(f32).astype(bf16)
             for slot in range(2):
                 mate = jnp.where(diagonal, slot, 1 - slot)
-                vectors = jnp.concatenate(
-                    [hits_right[mate, :, :, :, c].reshape(2048, BLK) for c in range(2)], axis=1
-                )
-                pieces = jnp.dot(left_t[slot] * chosen, vectors, preferred_element_type=f32)
-                weights[slot, t, 0] = (pieces[:BLK, :BLK] - pieces[BLK:, BLK:]).astype(bf16)
-                weights[slot, t, 1] = (pieces[:BLK, BLK:] + pieces[BLK:, :BLK]).astype(bf16)
+                vectors = jnp.concatenate([
+                    jnp.concatenate([hits_right[mate, order[n], :, :, c].reshape(512, BLK)
+                                     for n in planes], axis=0)
+                    for c in range(2)
+                ], axis=1)
+                pieces = jnp.dot(left_t[slot, :, span] * chosen, vectors,
+                                 preferred_element_type=f32)
+                values = (pieces[:BLK, :BLK] - pieces[BLK:, BLK:],
+                          pieces[:BLK, BLK:] + pieces[BLK:, :BLK])
+                for c in range(2):
+                    if first:
+                        partial[slot, t, c] = values[c]
+                    else:
+                        weights[slot, t, c] = (partial[slot, t, c] + values[c]).astype(bf16)
 
     def box(begin, end, later, shift):
         @pl.loop(begin, end)
@@ -512,11 +533,14 @@
     relay_refs = [hits_left.at[:, opposite], hits_right.at[:, opposite], hits_ids.at[opposite]]
     for n in range(3):
         landed(ring_refs[n], ring_recv.at[1, n])
-        landed(relay_refs[n], relay_recv.at[n])
-    left_vectors()
+    left_vectors((0, 1, 2))
+    add_weights((0, 1, 2), True)
     serve_products()
     pass_on(1)
-    all_weights()
+    for n in range(3):
+        landed(relay_refs[n], relay_recv.at[n])
+    left_vectors((3,))
+    add_weights((3,), False)
     for copy in kept:
         copy.wait()
     for slot in range(2):
@@ -563,10 +587,6 @@
 def on_device(field_codes, scales, mom_index, separations, source_slice, noise_left, noise_right):
     bf16, f32 = jnp.bfloat16, jnp.float32
     dma = pltpu.SemaphoreType.DMA
-    blocks = noise_left.reshape(64, 2, 8, BLK).transpose(2, 1, 0, 3)
-    own_blocks = noise_right.reshape(64, 2, 2, BLK).transpose(2, 1, 0, 3)
-    ids = jnp.broadcast_to(jnp.tile(source_slice.astype(bf16), 2), (16, BLK))
-
     any_spec = pl.BlockSpec(memory_space=ANY)
     smem = pl.BlockSpec(memory_space=pltpu.SMEM)
     vmem = pl.BlockSpec(memory_space=pltpu.VMEM)
@@ -574,9 +594,12 @@
     total = pl.pallas_call(
         contract,
         out_shape=jax.ShapeDtypeStruct((8, BLK), f32),
-        in_specs=[smem, smem, any_spec, vmem, any_spec, any_spec, any_spec],
+        in_specs=[smem, smem, any_spec, vmem, vmem, vmem, vmem],
         out_specs=vmem,
         scratch_shapes=[
+            dims(8, 2, 64, BLK),
+            dims(2, 2, 64, BLK),
+            dims(16, BLK),
             dims(2, 2, 2, 256, 1024),
             dims(2, 2, 1024, 1024),
             dims(2, 16, 2, 2, BLK, BLK),
@@ -596,6 +619,7 @@
             dims(4, 4, 2, 16, BLK),
             dims(2, 2 * BLK, 2048),
             pltpu.VMEM((16, 2048), f32),
+            pltpu.VMEM((2, SPAN, 2, BLK, BLK), f32),
             dims(2, SPAN, 2, BLK, BLK),
             pltpu.VMEM((3 * SPAN, 4, BLK), f32),
             pltpu.VMEM((3 * SPAN, 2, BLK), f32),
@@ -615,7 +639,10 @@
         ],
         compiler_params=params(0),
         name="contract",
-    )(mom_index, separations, field_codes, scales, blocks, own_blocks, ids)
+    )(
+        mom_index, separations, field_codes, scales, noise_left, noise_right,
+        source_slice.reshape(1, 64),
+    )
     mine = total[:6, :8].reshape(2, 3, 8)
     box = jnp.stack(
         [

time: 170 us -> 161 us (0.947)
  local copies, waits for them, and re-layouts: 6.87 us -> 2.77 us
  Pallas kernels: 161 us -> 157 us
    pallas_call x1, Pallas kernels: 161 us -> 157 us  [on_device(): pl.pallas_call(contract, out_shape=jax.ShapeDtypeStruct((8, BLK), f32), i...]
    reshape x4 -> x0, local copies, waits for them, and re-layouts: 3.4 us -> none  [the longest x2 1.88 us: on_device(): blocks = noise_left.reshape(64, 2, 8, BLK).transpose(2, 1, 0, 3)]
where the time goes in v7:
time: 161 us
  Pallas kernels  157 us (98%)
  local copies, waits for them, and re-layouts  2.77 us (2%)
    pallas_call x1, Pallas kernels, on_device(): pl.pallas_call(contract, out_shape=jax.ShapeDtypeStruct((8, BLK), f32), i...  157 us

profile of v7, /device:TPU:1, one launch (start us, length us, event | category | flops | bytes accessed | tf_op | source)
XLA Modules:
  0.0 160.9 jit_solution(7369144476093708565)
XLA Ops:
  0.6 157.4 %contract.1 = f32[8,128]{1,0:T(8,128)} custom-call(s32[4]{0:T(128)} %mom.1, s32[3]{0:T(128)} %seps.1, bf16[2,2,2,256,1024]{4,3,2,1,0:T(8,128)(2,1)} %codes.1, f32[2,2,256]{2,1,0:T(2,128)} %scales.1, bf16[64,2,1024]{2,1,0:T(2,128)(2,1)} %all_left.1, bf16[64,2,256]{2,1,0:T(2,128)(2,1)} %all_right.1, s32[1,64]{1,0:T(1,128)} %bitcast.3), custom_call_target="tpu_custom_call" | custom-call | tf_op jit(solution)/shard_map/contract/pallas_call | solution.py:594
  158.0 0.7 reshape.13
  158.7 0.1 multiply_subtract_fusion
  158.8 0.1 pad_maximum_fusion
  158.8 0.7 copy.13
  159.5 0.1 fusion
  159.6 0.7 copy.14
  160.3 0.7 copy.15

commit v8 on v7

--- a/solution.py
+++ b/solution.py
@@ -165,8 +165,8 @@
     def tile(n):
         return pl.ds(n * BLK if isinstance(n, int) else pl.multiple_of(n * BLK, BLK), BLK)
 
-    def rows_of(block):
-        return whole.at[:, :, pl.ds(pl.multiple_of(block * 256, 256), 256), :]
+    def rows_of(block, m):
+        return whole.at[m, :, pl.ds(pl.multiple_of(block * 256, 256), 256), :]
 
     assembly = []
     for s in range(2):
@@ -180,9 +180,9 @@
                     value = fields[m, s, c, :, tile(n)].astype(f32) * column
                     fields[m, s, c, :, tile(n)] = value.astype(bf16)
 
-        assembly.append(remote(fields.at[:, s], rows_of(me.mode), asm_send.at[s],
-                               asm_recv.at[me.hi], (flip, 2 * s + me.core)))
-        assembly[-1].start()
+            assembly.append(remote(fields.at[m, s], rows_of(me.mode, m), asm_send.at[s, m],
+                                   asm_recv.at[me.hi, m], (flip, 2 * s + me.core)))
+            assembly[-1].start()
 
     for ref, into, count in ((all_left, left, 8), (all_right, right, 2)):
         for c in range(2):
@@ -298,12 +298,13 @@
         serve(1, me.hi, t)
 
     forwards = []
-    for h in range(2):
-        block = rows_of(2 * h + me.core)
-        landed(block, asm_recv.at[h])
-        forwards.append(remote(block, block, fwd_send.at[h], fwd_recv.at[h],
-                               (me.tm, me.mode + 1 - 2 * me.core)))
-        forwards[-1].start()
+    for m in range(2):
+        for h in range(2):
+            block = rows_of(2 * h + me.core, m)
+            landed(block, asm_recv.at[h, m])
+            forwards.append(remote(block, block, fwd_send.at[h, m], fwd_recv.at[h, m],
+                                   (me.tm, me.mode + 1 - 2 * me.core)))
+            forwards[-1].start()
 
     for z in range(4):
         for group in range(2):
@@ -316,8 +317,9 @@
 
     start_ring()
 
-    for h in range(2):
-        landed(rows_of(2 * h + 1 - me.core), fwd_recv.at[h])
+    for m in range(2):
+        for h in range(2):
+            landed(rows_of(2 * h + 1 - me.core, m), fwd_recv.at[h, m])
     for hi in range(2):
         for z in range(4):
             pair = blocks_of(z, 1, hi, me.core)
@@ -626,7 +628,7 @@
             pltpu.VMEM((3 * SPAN, 2, BLK), f32),
             pltpu.VMEM((8, 8, BLK), f32),
             pltpu.VMEM((32, 8, BLK), f32),
-            dma((2,)), dma((2,)), dma((2,)), dma((2,)), dma((2,)),
+            dma((2,)), dma((2, 2)), dma((2, 2)), dma((2, 2)), dma((2, 2)),
             dma((4, 2)), dma((4, 2)), dma((2, 4)), dma((2, 4)), dma((2, 4, 2)),
             dma((4,)), dma((4,)), dma((4,)), dma((4,)), dma((4, 2)),
             dma((2, 2, 4)), dma((4, 4)), dma((4, 4)), dma((2, 4, 2)),

time: 161 us -> 161 us (level)
  no operation moved by 1% of the time
where the time goes in v8:
time: 161 us
  Pallas kernels  157 us (98%)
  local copies, waits for them, and re-layouts  2.77 us (2%)
    pallas_call x1, Pallas kernels, on_device(): pl.pallas_call(contract, out_shape=jax.ShapeDtypeStruct((8, BLK), f32), i...  157 us

profile of v8, /device:TPU:1, one launch (start us, length us, event | category | flops | bytes accessed | tf_op | source)
XLA Modules:
  0.0 160.6 jit_solution(16394904926308485169)
XLA Ops:
  0.6 157.0 %contract.1 = f32[8,128]{1,0:T(8,128)} custom-call(s32[4]{0:T(128)} %mom.1, s32[3]{0:T(128)} %seps.1, bf16[2,2,2,256,1024]{4,3,2,1,0:T(8,128)(2,1)} %codes.1, f32[2,2,256]{2,1,0:T(2,128)} %scales.1, bf16[64,2,1024]{2,1,0:T(2,128)(2,1)} %all_left.1, bf16[64,2,256]{2,1,0:T(2,128)(2,1)} %all_right.1, s32[1,64]{1,0:T(1,128)} %bitcast.3), custom_call_target="tpu_custom_call" | custom-call | tf_op jit(solution)/shard_map/contract/pallas_call | solution.py:596
  157.6 0.7 reshape.13
  158.3 0.1 multiply_subtract_fusion
  158.4 0.1 pad_maximum_fusion
  158.5 0.7 copy.13
  159.2 0.1 fusion
  159.2 0.7 copy.14
  159.9 0.7 copy.15
